TPU v7x, 512 devices: a whole 4x4x16 slice. The times are simulated.
512 devices in a mesh: depth: 16 (over z), lat: 32 (over x, y, core).
Axes of the slice: x: 4, y: 4, z: 16, core: 2. Of those that a mesh axis runs over, the one named last changes fastest.
Arguments:
- down_real: float32 [64, 256, 256], P('depth', 'lat'), may hold values from -6 to 6
- down_imaginary: float32 [64, 256, 256], P('depth', 'lat'), may hold values from -6 to 6
- up_real: float32 [64, 256, 256], P('depth', 'lat'), may hold values from -6 to 6
- up_imaginary: float32 [64, 256, 256], P('depth', 'lat'), may hold values from -6 to 6
- slowness: float32 [64, 256, 256], P('depth', 'lat'), may hold values from 0.7 to 1.4
- ref_slow: float32 [64], P('depth'), may hold values from 0.8 to 1.2
- reflectivity: float32 [64, 256, 256], P('depth', 'lat'), may hold values from -0.3 to 0.3
- source_real: float32 [256, 256], P('lat'), may hold values from -6 to 6
- source_imaginary: float32 [256, 256], P('lat'), may hold values from -6 to 6
Outputs:
- next_down_real: float32 [64, 256, 256], P('depth', 'lat')
- next_down_imaginary: float32 [64, 256, 256], P('depth', 'lat')
- next_up_real: float32 [64, 256, 256], P('depth', 'lat')
- next_up_imaginary: float32 [64, 256, 256], P('depth', 'lat')
All inputs are finite; a program needn't handle non-finite values.
Results may differ from a plain program's by a relative error of at most 0.0003.
Values sent between devices are 32-bit elements; how exact they have to be, the bound alone decides.
A program may use at most 64 MiB of HBM per device.

v0:
```python
import math

import jax
import jax.numpy as jnp
import ml_dtypes
import numpy as np
from jax import lax
from jax.experimental import pallas as pl
from jax.experimental.pallas import tpu as pltpu
from jax.sharding import PartitionSpec as P

TICKS = 3
OMEGA = 2.5
MESH = pl.DeviceIdType.MESH

LEVELS = 4
PLANES = 2 * LEVELS
LAT = 32
ROWS = 8
N = 256
LANES = 2 * PLANES * ROWS
HALF = LANES // 2


def split(x):
    high = x.astype(jnp.bfloat16)
    low = (x - high.astype(jnp.float32)).astype(jnp.bfloat16)
    return high, low


def np_split(x):
    x = np.asarray(x, np.float64)
    high = x.astype(np.float32).astype(ml_dtypes.bfloat16)
    low = (x - high.astype(np.float64)).astype(np.float32).astype(ml_dtypes.bfloat16)
    return high, low


def constants():
    index = np.arange(N)
    angle = 2.0 * np.pi * (np.outer(index, index) % N) / N
    cos_hi, cos_lo = np_split(np.cos(angle))
    sin_hi, sin_lo = np_split(np.sin(angle))
    full = np.stack([cos_hi, sin_hi, cos_lo, sin_lo])
    coarse = np.arange(LAT)
    angle = 2.0 * np.pi * (np.outer(coarse, coarse) % LAT) / LAT
    eye = np.eye(ROWS)
    both = np.concatenate([np.kron(np.cos(angle), eye), np.kron(np.sin(angle), eye)])
    outer = np.stack(np_split(both))
    fine = np.arange(ROWS)
    angle = 2.0 * np.pi * (np.outer(fine, fine) % ROWS) / ROWS
    cosine, sine = (np.kron(np.eye(PLANES), f(angle)) for f in (np.cos, np.sin))
    inner = []
    for sign in (1.0, -1.0):
        block = np.block([[cosine, -sign * sine], [sign * sine, cosine]])
        high, low = np_split(block)
        inner.append(np.block([[high, low], [high, low]]))
    inner = np.stack(inner)
    turn = 2.0 * np.pi * np.outer(coarse, fine) / N
    cosine = np.tile(np.cos(turn), (1, LANES // ROWS))
    sine = np.tile(np.sin(turn), (1, LANES // ROWS))
    sine[:, HALF:] *= -1.0
    twiddle = np.stack([cosine, sine]).astype(np.float32)[:, :, None, :]
    return full, outer, inner, twiddle


def dot(a, b, dims=((1,), (0,))):
    return lax.dot_general(a, b, (dims, ((), ())), preferred_element_type=jnp.float32)


def forward_y(real, imag, full):
    real_hi, real_lo = split(real)
    imag_hi, imag_lo = split(imag)
    same = jnp.concatenate([real_hi, imag_hi, real_lo, imag_lo], axis=0)
    swapped = jnp.concatenate([imag_hi, -real_hi, imag_lo, -real_lo], axis=0)
    last = ((1,), (1,))
    wide = dot(full[0], same, last) + dot(full[1], swapped, last)
    rest = dot(full[2], same[:LANES], last) + dot(full[3], swapped[:LANES], last)
    return wide[:, :LANES] + (wide[:, LANES:] + rest)


def signs(shape):
    lane = lax.broadcasted_iota(jnp.int32, shape, len(shape) - 1)
    return jnp.where(lane < HALF, 1.0, -1.0).astype(jnp.float32)


def outer_step(x, outer, sign, roll):
    high, low = split(x)
    wide = dot(outer[0], jnp.concatenate([high, low], axis=1))
    total = wide[:, :LANES] + (wide[:, LANES:] + dot(outer[1], high))
    return total[:N] + sign * roll(total[N:])


def inner_step(x, inner):
    high, low = split(x)
    wide = dot(jnp.concatenate([high, low], axis=1), inner)
    return wide[:, :LANES] + wide[:, LANES:]


def turned(x, cosine, sine, roll):
    return x * cosine + roll(x) * sine


def middle(x, mult_real, mult_imag, outer, inner, twiddle, roll):
    sign = signs((N, LANES))
    shape = (LAT, ROWS, LANES)
    cosine = jnp.broadcast_to(twiddle[0], shape).reshape(N, LANES)
    sine = jnp.broadcast_to(twiddle[1], shape).reshape(N, LANES)
    x = outer_step(x, outer, sign, roll)
    x = turned(x, cosine, sine, roll)
    x = inner_step(x, inner[0])
    x = turned(x, mult_real, mult_imag, roll)
    x = inner_step(x, inner[1])
    x = turned(x, cosine, -sine, roll)
    return outer_step(x, outer, -sign, roll)


def backward_y(x, full):
    high, low = split(x.T)
    both = jnp.concatenate([high, low], axis=0)
    cosine = dot(both, full[0])
    sine = dot(both, full[1])
    cosine = cosine[:LANES] + (cosine[LANES:] + dot(high, full[2]))
    sine = sine[:LANES] + (sine[LANES:] + dot(high, full[3]))
    return cosine[:HALF] - sine[HALF:], cosine[HALF:] + sine[:HALF]


def wrapped_numbers(index):
    folded = jnp.where(index < N // 2, index, index - N)
    return folded.astype(jnp.float32) * (2.0 * math.pi / N)


def multiplier(me, ref_slow):
    row = lax.broadcasted_iota(jnp.int32, (N, LANES), 0)
    lane = lax.broadcasted_iota(jnp.int32, (N, LANES), 1)
    wave_x = wrapped_numbers(row // ROWS + LAT * (lane % ROWS))
    wave_y = wrapped_numbers(ROWS * me + row % ROWS)
    level = (lane // ROWS) % LEVELS
    slow = jnp.full((N, LANES), ref_slow[0], jnp.float32)
    for z in range(1, LEVELS):
        slow = jnp.where(level == z, ref_slow[z], slow)
    argument = (OMEGA * slow) ** 2 - (wave_x * wave_x + wave_y * wave_y)
    vertical = jnp.sqrt(jnp.maximum(argument, 0.0))
    factor = jnp.exp(-jnp.sqrt(jnp.maximum(-argument, 0.0))) * (1.0 / (N * N))
    return factor * jnp.cos(vertical), signs((N, LANES)) * (factor * jnp.sin(vertical))


def kernel(
    down_real, down_imag, up_real, up_imag, slowness, ref_slow, reflect, source_real, source_imag,
    full_hbm, outer_hbm, inner_hbm, twiddle_hbm,
    out_dr, out_di, out_ur, out_ui,
    state, slow, refl, source, full, outer, inner, twiddle,
    mult, corr, send_there, send_back, got_there, got_back, edge_send, edge_got,
    in_sems, out_sems, there_send, there_recv, back_send, back_recv, edge_send_sems, edge_recv_sems,
):
    me = lax.axis_index("lat")
    depth = lax.axis_index("depth")
    depths = lax.axis_size("depth")
    below = lax.rem(depth + 1, depths)
    above = lax.rem(depth + depths - 1, depths)

    def roll(x):
        return pltpu.roll(x, HALF, 1)

    loads = [
        pltpu.make_async_copy(src, dst, in_sems.at[n])
        for n, (src, dst) in enumerate([
            (down_real, state.at[0, 0]), (up_real, state.at[0, 1]),
            (down_imag, state.at[1, 0]), (up_imag, state.at[1, 1]),
            (full_hbm, full), (outer_hbm, outer), (inner_hbm, inner), (twiddle_hbm, twiddle),
            (slowness, slow), (reflect, refl), (source_real, source.at[0]), (source_imag, source.at[1]),
        ])
    ]
    for load in loads:
        load.start()

    barrier = pltpu.get_barrier_semaphore()

    def greet(step, _):
        pl.semaphore_signal(
            barrier, inc=1, device_id=(depth, lax.rem(me + step, LAT)), device_id_type=MESH
        )
        return 0

    lax.fori_loop(1, LAT, greet, 0)
    for neighbour in (above, below):
        pl.semaphore_signal(barrier, inc=1, device_id=(neighbour, me), device_id_type=MESH)
    for load in loads[:5]:
        load.wait()

    def exchange(tick, sent, got, send_sems, recv_sems):
        def send(step, _):
            peer = lax.rem(me + step, LAT)
            pltpu.make_async_remote_copy(
                src_ref=sent.at[tick, peer],
                dst_ref=got.at[tick, me],
                send_sem=send_sems.at[tick],
                recv_sem=recv_sems.at[tick],
                device_id=(depth, peer),
                device_id_type=MESH,
            ).start()
            return 0

        lax.fori_loop(1, LAT, send, 0)
        got[tick, me] = sent[tick, me]
        return pltpu.make_async_remote_copy(
            src_ref=sent.at[tick, pl.ds(0, LAT - 1)],
            dst_ref=got.at[tick, pl.ds(0, LAT - 1)],
            send_sem=send_sems.at[tick],
            recv_sem=recv_sems.at[tick],
            device_id=(depth, lax.rem(me + 1, LAT)),
            device_id_type=MESH,
        )

    def edge(tick, which, target):
        return pltpu.make_async_remote_copy(
            src_ref=edge_send.at[tick, which],
            dst_ref=edge_got.at[tick, which],
            send_sem=edge_send_sems.at[tick, which],
            recv_sem=edge_recv_sems.at[tick, which],
            device_id=(target, me),
            device_id_type=MESH,
        )

    def one_tick(tick, _):
        real = state[0].reshape(PLANES * ROWS, N)
        imag = state[1].reshape(PLANES * ROWS, N)
        send_there[tick] = forward_y(real, imag, full).reshape(LAT, ROWS, LANES)

        @pl.when(tick == 0)
        def _():
            pl.semaphore_wait(barrier, LAT + 1)

        there = exchange(tick, send_there, got_there, there_send, there_recv)

        @pl.when(tick == 0)
        def _():
            for load in loads[5:]:
                load.wait()
            mult[0], mult[1] = multiplier(me, ref_slow)

        there.wait_recv()
        x = got_there[tick].reshape(N, LANES)
        x = middle(x, mult[0], mult[1], outer, inner, twiddle, roll)
        send_back[tick] = x.reshape(LAT, ROWS, LANES)
        back = exchange(tick, send_back, got_back, back_send, back_recv)

        @pl.when(tick == 0)
        def _():
            for z in range(LEVELS):
                theta = OMEGA * (slow[z] - ref_slow[z])
                corr[0, z] = jnp.cos(theta)
                corr[1, z] = jnp.sin(theta)

        back.wait_recv()
        real, imag = backward_y(got_back[tick].reshape(N, LANES), full)
        real = real.reshape(2, LEVELS, ROWS, N)
        imag = imag.reshape(2, LEVELS, ROWS, N)
        prop_real = real * corr[0] + imag * corr[1]
        prop_imag = imag * corr[0] - real * corr[1]
        edge_send[tick, 0, 0] = prop_real[0, LEVELS - 1]
        edge_send[tick, 0, 1] = prop_imag[0, LEVELS - 1]
        edge_send[tick, 1, 0] = prop_real[1, 0]
        edge_send[tick, 1, 1] = prop_imag[1, 0]
        edges = [edge(tick, 0, below), edge(tick, 1, above)]
        for one in edges:
            one.start()
        is_top = depth == 0
        is_bottom = depth == depths - 1
        for part, prop in enumerate((prop_real, prop_imag)):
            for z in range(1, LEVELS - 1):
                state[part, 0, z] = prop[0, z - 1] - refl[z] * prop[1, z + 1]
                state[part, 1, z] = prop[1, z + 1] + refl[z] * prop[0, z - 1]
        for one in edges:
            one.wait_recv()
        last = LEVELS - 1
        for part, prop in enumerate((prop_real, prop_imag)):
            head = jnp.where(is_top, source[part], edge_got[tick, 0, part])
            tail = jnp.where(is_bottom, 0.0, edge_got[tick, 1, part])
            state[part, 0, 0] = head - refl[0] * prop[1, 1]
            state[part, 1, 0] = prop[1, 1] + refl[0] * head
            state[part, 0, last] = prop[0, last - 1] - refl[last] * tail
            state[part, 1, last] = tail + refl[last] * prop[0, last - 1]
        there.wait_send()
        back.wait_send()
        for one in edges:
            one.wait_send()
        return 0

    lax.fori_loop(0, TICKS, one_tick, 0)
    stores = [
        pltpu.make_async_copy(src, dst, out_sems.at[n])
        for n, (src, dst) in enumerate([
            (state.at[0, 0], out_dr), (state.at[1, 0], out_di),
            (state.at[0, 1], out_ur), (state.at[1, 1], out_ui),
        ])
    ]
    for store in stores:
        store.start()
    for store in stores:
        store.wait()


def solution(mesh):
    consts = constants()
    plane = jax.ShapeDtypeStruct((LEVELS, ROWS, N), jnp.float32)
    anywhere = pl.BlockSpec(memory_space=pl.ANY)
    smem = pl.BlockSpec(memory_space=pltpu.SMEM)
    f32 = jnp.float32

    def step(*args):
        return pl.pallas_call(
            kernel,
            out_shape=[plane] * 4,
            in_specs=[anywhere] * 5 + [smem] + [anywhere] * 7,
            out_specs=[anywhere] * 4,
            scratch_shapes=[
                pltpu.VMEM((2, 2, LEVELS, ROWS, N), f32),
                pltpu.VMEM((LEVELS, ROWS, N), f32),
                pltpu.VMEM((LEVELS, ROWS, N), f32),
                pltpu.VMEM((2, ROWS, N), f32),
                *[pltpu.VMEM(c.shape, c.dtype) for c in consts],
                pltpu.VMEM((2, N, LANES), f32),
                pltpu.VMEM((2, LEVELS, ROWS, N), f32),
                *[pltpu.VMEM((TICKS, LAT, ROWS, LANES), f32)] * 4,
                *[pltpu.VMEM((TICKS, 2, 2, ROWS, N), f32)] * 2,
                pltpu.SemaphoreType.DMA((12,)),
                pltpu.SemaphoreType.DMA((4,)),
                *[pltpu.SemaphoreType.DMA((TICKS,))] * 4,
                *[pltpu.SemaphoreType.DMA((TICKS, 2))] * 2,
            ],
            compiler_params=pltpu.CompilerParams(
                collective_id=0, has_side_effects=True, vmem_limit_bytes=32 * 2**20
            ),
        )(*args, *[jnp.asarray(c) for c in consts])

    lateral = P("depth", "lat", None)
    return jax.shard_map(
        step,
        mesh=mesh,
        in_specs=(lateral,) * 5 + (P("depth"), lateral, P("lat", None), P("lat", None)),
        out_specs=(lateral,) * 4,
        check_vma=False,
    )
```

profile of v0, /device:TPU:1, one launch (start us, length us, event | category | flops | bytes accessed | tf_op | source)
XLA Modules:
  0.0 76.2 jit_solution(10520301653732209727)
XLA Ops:
  0.6 0.0 copy-start
  0.6 1.0 %copy-done = bf16[2,512,256]{2,1,0:T(8,128)(2,1)S(1)} copy-done((bf16[2,512,256]{2,1,0:T(8,128)(2,1)S(1)}, bf16[2,512,256]{2,1,0:T(8,128)(2,1)}, u32[]{:S(2)}) %copy-start) | copy-done | bytes 524312
  1.7 0.0 copy-start.1
  1.7 1.0 %copy-done.1 = bf16[4,256,256]{2,1,0:T(8,128)(2,1)S(1)} copy-done((bf16[4,256,256]{2,1,0:T(8,128)(2,1)S(1)}, bf16[4,256,256]{2,1,0:T(8,128)(2,1)}, u32[]{:S(2)}) %copy-start.1) | copy-done | bytes 524312
  2.7 0.0 copy-start.2
  2.7 0.9 %copy-done.2 = bf16[2,256,256]{2,1,0:T(8,128)(2,1)S(1)} copy-done((bf16[2,256,256]{2,1,0:T(8,128)(2,1)S(1)}, bf16[2,256,256]{2,1,0:T(8,128)(2,1)}, u32[]{:S(2)}) %copy-start.2) | copy-done | bytes 262168
  3.7 0.0 copy-start.3
  3.7 0.8 copy-done.3
  4.4 0.0 copy-start.4
  4.4 0.8 copy-done.4
  5.2 0.0 copy-start.5
  5.2 0.8 copy-done.5
  5.9 0.0 copy-start.6
  5.9 0.8 copy-done.6
  6.7 0.0 copy-start.7
  6.7 0.8 copy-done.7
  7.5 0.0 copy-start.8
  7.5 0.8 copy-done.8
  8.2 0.0 copy-start.9
  8.2 0.8 copy-done.9
  9.0 0.0 copy-start.10
  9.0 0.7 copy-done.10
  9.7 0.0 copy-start.11
  9.7 0.7 copy-done.11
  10.4 0.0 copy-start.12
  10.4 0.7 copy-done.12
  11.0 62.7 %shard_map.156 = (f32[4,8,256]{2,1,0:T(8,128)S(1)}, f32[4,8,256]{2,1,0:T(8,128)S(1)}, f32[4,8,256]{2,1,0:T(8,128)S(1)}, f32[4,8,256]{2,1,0:T(8,128)S(1)}) custom-call(f32[4,8,256]{2,1,0:T(8,128)S(1)} %copy-done.3, f32[4,8,256]{2,1,0:T(8,128)S(1)} %copy-done.4, f32[4,8,256]{2,1,0:T(8,128)S(1)} %copy-done.5, f32[4,8,256]{2,1,0:T(8,128)S(1)} %copy-done.6, ...), custom_call_target="tpu_custom_call" | custom-call | tf_op jit(solution)/shard_map/pallas_call | solution.py:311
  73.7 0.6 copy.21
  74.4 0.6 copy.22
  75.0 0.6 copy.23
  75.6 0.6 copy.24
Async XLA Ops:
  0.6 1.0 %copy-start = (bf16[2,512,256]{2,1,0:T(8,128)(2,1)S(1)}, bf16[2,512,256]{2,1,0:T(8,128)(2,1)}, u32[]{:S(2)}) copy-start(bf16[2,512,256]{2,1,0:T(8,128)(2,1)} %constant.9.clone.outer_hbm) | copy-start | bytes 1572868
  1.7 1.0 %copy-start.1 = (bf16[4,256,256]{2,1,0:T(8,128)(2,1)S(1)}, bf16[4,256,256]{2,1,0:T(8,128)(2,1)}, u32[]{:S(2)}) copy-start(bf16[4,256,256]{2,1,0:T(8,128)(2,1)} %constant.8.clone.full_hbm) | copy-start | bytes 1572868
  2.7 0.9 %copy-start.2 = (bf16[2,256,256]{2,1,0:T(8,128)(2,1)S(1)}, bf16[2,256,256]{2,1,0:T(8,128)(2,1)}, u32[]{:S(2)}) copy-start(bf16[2,256,256]{2,1,0:T(8,128)(2,1)} %constant.10.clone.inner_hbm) | copy-start | bytes 786436
  3.7 0.8 copy-start.3
  4.4 0.8 copy-start.4
  5.2 0.8 copy-start.5
  5.9 0.8 copy-start.6
  6.7 0.8 copy-start.7
  7.5 0.8 copy-start.8
  8.2 0.8 copy-start.9
  9.0 0.7 copy-start.10
  9.7 0.7 copy-start.11
  10.4 0.7 copy-start.12
where the time goes:
time: 77 us; the launch traced here: 76.2 us
  Pallas kernels  62.7 us (81%)
  local copies, waits for them, and re-layouts  12.8 us (17%)
    pallas_call x1, Pallas kernels, step(): pl.pallas_call(kernel, out_shape=[plane] * 4, in_specs=[anywhere] * 5 + [...  62.7 us
    unnamed x30, local copies, waits for them, and re-layouts  12.8 us

commit v1 on v0

v1 whole, which is shorter than its diff:
```python
import math

import jax
import jax.numpy as jnp
import ml_dtypes
import numpy as np
from jax import lax
from jax.experimental import pallas as pl
from jax.experimental.pallas import tpu as pltpu
from jax.sharding import PartitionSpec as P

TICKS = 3
OMEGA = 2.5
MESH = pl.DeviceIdType.MESH

LEVELS = 4
GROUP = 8
LAT = 32
ROWS = 8
N = 256
LANES = 128
HALF = 64
SLOT = 16


def split(x):
    high = x.astype(jnp.bfloat16)
    low = (x - high.astype(jnp.float32)).astype(jnp.bfloat16)
    return high, low


def np_split(x):
    x = np.asarray(x, np.float64)
    high = x.astype(np.float32).astype(ml_dtypes.bfloat16)
    low = (x - high.astype(np.float64)).astype(np.float32).astype(ml_dtypes.bfloat16)
    return high, low


def constants():
    index = np.arange(N)
    slot, device, row = np.meshgrid(np.arange(LEVELS), np.arange(GROUP), np.arange(ROWS), indexing="ij")
    waves = (LAT * device + ROWS * slot + row).reshape(-1)
    angle = 2.0 * np.pi * (np.outer(waves, index) % N) / N
    cos_hi, cos_lo = np_split(np.cos(angle))
    sin_hi, sin_lo = np_split(np.sin(angle))
    full = np.stack([cos_hi, sin_hi, cos_lo, sin_lo])
    coarse = np.arange(LAT)
    angle = 2.0 * np.pi * (np.outer(coarse, coarse) % LAT) / LAT
    eye = np.eye(ROWS)
    both = np.concatenate([np.kron(np.cos(angle), eye), np.kron(np.sin(angle), eye)])
    outer = np.stack(np_split(both))
    fine = np.arange(ROWS)
    angle = 2.0 * np.pi * (np.outer(fine, fine) % ROWS) / ROWS
    cosine, sine = (np.kron(np.eye(HALF // ROWS), f(angle)) for f in (np.cos, np.sin))
    inner = []
    for sign in (1.0, -1.0):
        block = np.block([[cosine, -sign * sine], [sign * sine, cosine]])
        high, low = np_split(block)
        inner.append(np.block([[high, low], [high, low]]))
    inner = np.stack(inner)
    turn = 2.0 * np.pi * np.outer(coarse, fine) / N
    cosine = np.tile(np.cos(turn), (1, LANES // ROWS))
    sine = np.tile(np.sin(turn), (1, LANES // ROWS))
    sine[:, HALF:] *= -1.0
    twiddle = np.stack([cosine, sine]).astype(np.float32)[:, :, None, :]
    return full, outer, inner, twiddle


def dot(a, b, dims=((1,), (0,))):
    return lax.dot_general(a, b, (dims, ((), ())), preferred_element_type=jnp.float32)


def lanes(shape):
    return lax.broadcasted_iota(jnp.int32, shape, len(shape) - 1)


def slot_swap(tiles, roll):
    slot = (lanes(tiles[0].shape) // SLOT) % LEVELS
    for bit in (2, 1):
        keep = (slot & bit) == 0
        shift = bit * SLOT
        new = list(tiles)
        for a in range(LEVELS):
            if a & bit == 0:
                low, high = tiles[a], tiles[a + bit]
                new[a] = jnp.where(keep, low, roll(high, shift))
                new[a + bit] = jnp.where(keep, roll(low, LANES - shift), high)
        tiles = new
    return tiles


def forward_y(real, imag, full, roll):
    real_hi, real_lo = split(real)
    imag_hi, imag_lo = split(imag)
    same = jnp.concatenate([real_hi, imag_hi, real_lo, imag_lo], axis=0)
    swapped = jnp.concatenate([imag_hi, -real_hi, imag_lo, -real_lo], axis=0)
    last = ((1,), (1,))
    wide = dot(full[0], same, last) + dot(full[1], swapped, last)
    rest = dot(full[2], same[:LANES], last) + dot(full[3], swapped[:LANES], last)
    total = wide[:, :LANES] + (wide[:, LANES:] + rest)
    return slot_swap([total[HALF * a : HALF * (a + 1)] for a in range(LEVELS)], roll)


def signs(shape):
    return jnp.where(lanes(shape) < HALF, 1.0, -1.0).astype(jnp.float32)


def outer_step(x, outer, sign, roll):
    high, low = split(x)
    wide = dot(outer[0], jnp.concatenate([high, low], axis=1))
    total = wide[:, :LANES] + (wide[:, LANES:] + dot(outer[1], high))
    return total[:N] + sign * roll(total[N:], HALF)


def inner_step(x, inner):
    high, low = split(x)
    wide = dot(jnp.concatenate([high, low], axis=1), inner)
    return wide[:, :LANES] + wide[:, LANES:]


def turned(x, cosine, sine, roll):
    return x * cosine + roll(x, HALF) * sine


def middle(x, mult_real, mult_imag, outer, inner, twiddle, roll):
    sign = signs((N, LANES))
    shape = (LAT, ROWS, LANES)
    cosine = jnp.broadcast_to(twiddle[0], shape).reshape(N, LANES)
    sine = jnp.broadcast_to(twiddle[1], shape).reshape(N, LANES)
    x = outer_step(x, outer, sign, roll)
    x = turned(x, cosine, sine, roll)
    x = inner_step(x, inner[0])
    x = turned(x, mult_real, mult_imag, roll)
    x = inner_step(x, inner[1])
    x = turned(x, cosine, -sine, roll)
    return outer_step(x, outer, -sign, roll)


def is_down(shape):
    return (lanes(shape) // ROWS) % 2 == 0


def packed(even, odd, roll):
    down = is_down(even.shape)
    return jnp.where(down, even, roll(odd, ROWS)), jnp.where(down, roll(even, LANES - ROWS), odd)


def backward_y(tiles, full, roll):
    x = jnp.concatenate(slot_swap(tiles, roll), axis=0)
    high, low = split(x.T)
    both = jnp.concatenate([high, low], axis=0)
    cosine = dot(both, full[0])
    sine = dot(both, full[1])
    cosine = cosine[:LANES] + (cosine[LANES:] + dot(high, full[2]))
    sine = sine[:LANES] + (sine[LANES:] + dot(high, full[3]))
    return cosine[:HALF] - sine[HALF:], cosine[HALF:] + sine[:HALF]


def wrapped_numbers(index):
    folded = jnp.where(index < N // 2, index, index - N)
    return folded.astype(jnp.float32) * (2.0 * math.pi / N)


def multiplier(member, slow):
    row = lax.broadcasted_iota(jnp.int32, (N, LANES), 0)
    lane = lax.broadcasted_iota(jnp.int32, (N, LANES), 1)
    wave_x = wrapped_numbers(row // ROWS + LAT * (lane % ROWS))
    wave_y = wrapped_numbers(LAT * member + ROWS * ((lane // SLOT) % LEVELS) + row % ROWS)
    argument = (OMEGA * slow) ** 2 - (wave_x * wave_x + wave_y * wave_y)
    vertical = jnp.sqrt(jnp.maximum(argument, 0.0))
    factor = jnp.exp(-jnp.sqrt(jnp.maximum(-argument, 0.0))) * (1.0 / (N * N))
    return factor * jnp.cos(vertical), signs((N, LANES)) * (factor * jnp.sin(vertical))


def mixed(real, imag, corr, refl, heads, tails, source):
    out = []
    for part in range(2):
        if part == 0:
            prop = real * corr[0] + imag * corr[1]
        else:
            prop = imag * corr[0] - real * corr[1]
        down = jnp.where(heads, source[part], prop[0])
        up = jnp.where(tails, 0.0, prop[1])
        out.append((down - refl * up, up + refl * down))
    return out


def kernel(
    down_real, down_imag, up_real, up_imag, slowness, ref_slow, reflect, source_real, source_imag,
    full_hbm, outer_hbm, inner_hbm, twiddle_hbm,
    out_dr, out_di, out_ur, out_ui,
    state, slow, source, full, outer, inner, twiddle,
    mult, context, corr, sent_there, got_there, sent_back, got_back, got_last, tiles, edge_sent, edge_got,
    in_sems, out_sems, there_send, there_recv, back_send, back_recv, last_send, last_recv,
    edge_send, edge_recv, context_send, context_recv, source_send, source_recv,
):
    me = lax.axis_index("lat")
    depth = lax.axis_index("depth")
    depths = lax.axis_size("depth")
    member = lax.rem(me, GROUP)
    column = me // GROUP
    flipped = lax.rem(depth, 2)
    level = jnp.where(flipped == 1, LEVELS - 1 - column, column)
    has_above = depth > 0
    has_below = depth < depths - 1
    last = TICKS - 1

    def column_of(z):
        return jnp.where(flipped == 1, LEVELS - 1 - z, z)

    def roll(x, shift):
        return pltpu.roll(x, shift, x.ndim - 1)

    def remote(src, dst, send_sem, recv_sem, where):
        return pltpu.make_async_remote_copy(
            src_ref=src, dst_ref=dst, send_sem=send_sem, recv_sem=recv_sem,
            device_id=where, device_id_type=MESH,
        )

    neighbour = (depth, lax.bitwise_xor(me, 1))

    loads = [
        pltpu.make_async_copy(src, dst, in_sems.at[n])
        for n, (src, dst) in enumerate([
            (down_real, state.at[0, :, 0]), (up_real, state.at[0, :, 1]),
            (down_imag, state.at[1, :, 0]), (up_imag, state.at[1, :, 1]),
            (full_hbm, full), (outer_hbm, outer), (inner_hbm, inner), (twiddle_hbm, twiddle),
            (slowness, slow), (reflect, context.at[1, :, 2]),
            (source_real, source.at[0, 0]), (source_imag, source.at[0, 1]),
        ])
    ]
    for load in loads:
        load.start()

    barrier = pltpu.get_barrier_semaphore()

    def greet(step, _):
        pl.semaphore_signal(
            barrier, inc=1, device_id=(depth, lax.bitwise_xor(me, step)), device_id_type=MESH
        )
        return 0

    lax.fori_loop(1, LAT, greet, 0)

    @pl.when(has_above)
    def _():
        pl.semaphore_signal(barrier, inc=1, device_id=(depth - 1, me), device_id_type=MESH)

    @pl.when(has_below)
    def _():
        pl.semaphore_signal(barrier, inc=1, device_id=(depth + 1, me), device_id_type=MESH)

    for load in loads[:5]:
        load.wait()

    def first_there():
        pl.semaphore_wait(barrier, LAT - 1 + has_above.astype(jnp.int32) + has_below.astype(jnp.int32))

        def send(step, _):
            peer = lax.bitwise_xor(me, step)
            remote(
                sent_there.at[0, lax.rem(peer, GROUP), column_of(peer // GROUP)],
                got_there.at[0, me], there_send.at[0], there_recv.at[0], (depth, peer),
            ).start()
            return 0

        lax.fori_loop(1, LAT, send, 0)
        got_there[0, me] = sent_there[0, member, level]
        for load in loads[8:]:
            load.wait()
        for z in range(LEVELS):
            slow[z] = OMEGA * (slow[z] - ref_slow[z])
        edge_sent[0] = slow[LEVELS - 1]
        edge_sent[1] = slow[0]
        down = remote(edge_sent.at[0], edge_got.at[0], edge_send.at[0], edge_recv.at[0], (depth + 1, me))
        up = remote(edge_sent.at[1], edge_got.at[1], edge_send.at[1], edge_recv.at[1], (depth - 1, me))

        @pl.when(has_below)
        def _():
            down.start()

        @pl.when(has_above)
        def _():
            up.start()

        for z in range(LEVELS - 1):
            context[1, z + 1, 0] = slow[z]
            context[1, z, 1] = slow[z + 1]
        mine = ref_slow[0]
        for z in range(1, LEVELS):
            mine = jnp.where(level == z, ref_slow[z], mine)
        for load in loads[5:8]:
            load.wait()
        mult[0], mult[1] = multiplier(member, mine)
        nothing = jnp.zeros((ROWS, N), jnp.float32)

        @pl.when(has_above)
        def _():
            down.wait_recv()
            context[1, 0, 0] = edge_got[0]

        @pl.when(jnp.logical_not(has_above))
        def _():
            context[1, 0, 0] = nothing

        @pl.when(has_below)
        def _():
            up.wait_recv()
            context[1, LEVELS - 1, 1] = edge_got[1]

        @pl.when(jnp.logical_not(has_below))
        def _():
            context[1, LEVELS - 1, 1] = nothing

        holder = me // LEVELS
        place = lax.rem(me, LEVELS)
        for z in range(LEVELS):
            target = column_of(z) * GROUP + holder

            @pl.when(target != me)
            def _():
                remote(
                    context.at[1, z], context.at[0, place], context_send, context_recv, (depth, target)
                ).start()

            @pl.when(target == me)
            def _():
                context[0, place] = context[1, z]

        @pl.when(jnp.logical_not(has_above))
        def _():
            @pl.when(holder != me)
            def _():
                remote(
                    source.at[0], source.at[1 + place], source_send, source_recv, (depth, holder)
                ).start()

            @pl.when(holder == me)
            def _():
                source[1 + place] = source[0]

    def later_there(tick):
        def send(step, _):
            peer = lax.bitwise_xor(member, step)
            remote(
                sent_there.at[tick, peer], got_there.at[tick, pl.ds(LEVELS * member, LEVELS)],
                there_send.at[tick], there_recv.at[tick], (depth, column * GROUP + peer),
            ).start()
            return 0

        lax.fori_loop(1, GROUP, send, 0)
        got_there[tick, pl.ds(LEVELS * member, LEVELS)] = sent_there[tick, member]

    def group_back(tick):
        forth = jnp.where(flipped == 1, -1, 1)
        is_last = level == LEVELS - 1
        is_first = level == 0
        down_to = (
            depth + is_last.astype(jnp.int32), (column + jnp.where(is_last, 0, forth)) * GROUP,
        )
        up_to = (
            depth - is_first.astype(jnp.int32), (column - jnp.where(is_first, 0, forth)) * GROUP,
        )
        goes_down = jnp.logical_or(has_below, jnp.logical_not(is_last))
        goes_up = jnp.logical_or(has_above, jnp.logical_not(is_first))
        sides = ((0, goes_down, down_to), (1, goes_up, up_to))
        for side, goes, (to_depth, base) in sides:
            @pl.when(goes)
            def _():
                def send(step, _):
                    peer = lax.bitwise_xor(member, step)
                    remote(
                        sent_back.at[tick, pl.ds(LAT // 2 * side + 2 * peer, 2)],
                        got_back.at[tick, side, pl.ds(2 * member, 2)],
                        back_send.at[tick, side], back_recv.at[tick, side], (to_depth, base + peer),
                    ).start()
                    return 0

                lax.fori_loop(0, GROUP, send, 0)
        return sides

    def group_back_waits(tick, side):
        return remote(
            sent_back.at[tick, pl.ds(LAT // 2 * side, LAT // 2)], got_back.at[tick, side],
            back_send.at[tick, side], back_recv.at[tick, side], neighbour,
        )

    def last_waits(side, count, to):
        return remote(
            sent_back.at[last, pl.ds(0, count)], got_last.at[pl.ds(to, count)],
            last_send.at[side], last_recv.at[side], neighbour,
        )

    def one_tick(tick, _):
        real = state[0].reshape(HALF, N)
        imag = state[1].reshape(HALF, N)
        for g, x in enumerate(forward_y(real, imag, full, roll)):
            sent_there[tick, :, g] = x.reshape(GROUP, ROWS, LANES)

        @pl.when(tick == 0)
        def _():
            first_there()
            remote(
                got_there.at[0, pl.ds(0, LAT - 1)], got_there.at[0, pl.ds(0, LAT - 1)],
                there_send.at[0], there_recv.at[0], neighbour,
            ).wait_recv()

        @pl.when(tick > 0)
        def _():
            later_there(tick)
            remote(
                got_there.at[tick, pl.ds(0, LAT - LEVELS)],
                got_there.at[tick, pl.ds(0, LAT - LEVELS)],
                there_send.at[tick], there_recv.at[tick], neighbour,
            ).wait_recv()

        x = got_there[tick].reshape(N, LANES)
        x = middle(x, mult[0], mult[1], outer, inner, twiddle, roll).reshape(LAT, ROWS, LANES)

        @pl.when(tick < last)
        def _():
            pairs = x.reshape(LAT // 2, 2, ROWS, LANES)
            down, up = packed(pairs[:, 0], pairs[:, 1], roll)
            sent_back[tick, : LAT // 2] = down
            sent_back[tick, LAT // 2 :] = up
            sides = group_back(tick)

            def fill(which):
                angle = context[which, :, 0:2]
                corr[which, 0] = jnp.cos(angle)
                corr[which, 1] = jnp.sin(angle)

            @pl.when(tick == 0)
            def _():
                holder = member * LEVELS
                here = jnp.logical_and(me >= holder, me < holder + LEVELS)
                for count in (LEVELS - 1, LEVELS):
                    @pl.when(here == (count < LEVELS))
                    def _():
                        remote(
                            context.at[1, pl.ds(0, count)], context.at[0, pl.ds(0, count)],
                            context_send, context_recv, neighbour,
                        ).wait_recv()

                    @pl.when(jnp.logical_and(jnp.logical_not(has_above), column == 0))
                    def _():
                        @pl.when(here == (count < LEVELS))
                        def _():
                            remote(
                                source.at[pl.ds(0, count)], source.at[pl.ds(1, count)],
                                source_send, source_recv, neighbour,
                            ).wait_recv()

                fill(0)

            @pl.when(tick == 1)
            def _():
                fill(1)

            comes_down = jnp.logical_or(has_above, level > 0)
            comes_up = jnp.logical_or(has_below, level < LEVELS - 1)
            for side, comes in ((0, comes_down), (1, comes_up)):
                @pl.when(comes)
                def _():
                    group_back_waits(tick, side).wait_recv()

                @pl.when(jnp.logical_not(comes))
                def _():
                    got_back[tick, side] = jnp.zeros((LAT // 2, ROWS, LANES), jnp.float32)

            down = got_back[tick, 0].reshape(GROUP, 2, ROWS, LANES)
            up = got_back[tick, 1].reshape(GROUP, 2, ROWS, LANES)
            for j in range(2):
                tiles[2 * j], tiles[2 * j + 1] = packed(down[:, j], up[:, j], roll)
            for side, goes, _ in sides:
                @pl.when(goes)
                def _():
                    group_back_waits(tick, side).wait_send()

        @pl.when(tick == last)
        def _():
            sent_back[last] = x
            slot = level * GROUP + member

            def send(step, _):
                peer = lax.bitwise_xor(me, step)
                remote(
                    sent_back.at[last, peer], got_last.at[slot],
                    last_send.at[0], last_recv.at[0], (depth, peer),
                ).start()
                return 0

            def send_past(side, where, place):
                def send(step, _):
                    peer = lax.bitwise_xor(me, step)
                    remote(
                        sent_back.at[last, peer], got_last.at[place + member],
                        last_send.at[side], last_recv.at[side], (where, peer),
                    ).start()
                    return 0

                lax.fori_loop(0, LAT, send, 0)

            goes_down = jnp.logical_and(level == LEVELS - 1, has_below)
            goes_up = jnp.logical_and(level == 0, has_above)

            @pl.when(goes_down)
            def _():
                send_past(1, depth + 1, LAT)

            @pl.when(goes_up)
            def _():
                send_past(2, depth - 1, LAT + GROUP)

            lax.fori_loop(1, LAT, send, 0)
            got_last[slot] = sent_back[last, me]
            for side, comes, place in ((1, has_above, LAT), (2, has_below, LAT + GROUP)):
                @pl.when(comes)
                def _():
                    last_waits(side, GROUP, place).wait_recv()

                @pl.when(jnp.logical_not(comes))
                def _():
                    got_last[pl.ds(place, GROUP)] = jnp.zeros((GROUP, ROWS, LANES), jnp.float32)

            last_waits(0, LAT - 1, 0).wait_recv()
            down = is_down((GROUP, ROWS, LANES))
            for z in range(LEVELS):
                above = GROUP * (z - 1) if z > 0 else LAT
                below = GROUP * (z + 1) if z < LEVELS - 1 else LAT + GROUP
                tiles[z] = jnp.where(
                    down, got_last[above : above + GROUP], got_last[below : below + GROUP]
                )
            last_waits(0, LAT - 1, 0).wait_send()
            for side, goes in ((1, goes_down), (2, goes_up)):
                @pl.when(goes)
                def _():
                    last_waits(side, LAT, 0).wait_send()

        real, imag = backward_y([tiles[g].reshape(HALF, LANES) for g in range(LEVELS)], full, roll)
        real = real.reshape(LEVELS, 2, ROWS, N)
        imag = imag.reshape(LEVELS, 2, ROWS, N)
        at_end = (tick == last).astype(jnp.int32)
        for g in range(LEVELS):
            heads = jnp.logical_and(jnp.logical_not(has_above), jnp.where(tick == last, g, level) == 0)
            tails = jnp.logical_and(
                jnp.logical_not(has_below), jnp.where(tick == last, g, level) == LEVELS - 1
            )
            origin = source[jnp.where(tick == last, 0, 1 + g)]
            parts = mixed(
                real[g], imag[g], corr[at_end, :, g], context[at_end, g, 2], heads, tails, origin
            )
            for part in range(2):
                state[part, g, 0], state[part, g, 1] = parts[part]
        return 0

    lax.fori_loop(0, TICKS, one_tick, 0)
    stores = [
        pltpu.make_async_copy(src, dst, out_sems.at[n])
        for n, (src, dst) in enumerate([
            (state.at[0, :, 0], out_dr), (state.at[1, :, 0], out_di),
            (state.at[0, :, 1], out_ur), (state.at[1, :, 1], out_ui),
        ])
    ]
    for store in stores:
        store.start()

    remote(
        got_there.at[0, pl.ds(0, LAT - 1)], got_there.at[0, pl.ds(0, LAT - 1)],
        there_send.at[0], there_recv.at[0], neighbour,
    ).wait_send()
    for tick in range(1, TICKS):
        remote(
            got_there.at[tick, pl.ds(0, LAT - LEVELS)], got_there.at[tick, pl.ds(0, LAT - LEVELS)],
            there_send.at[tick], there_recv.at[tick], neighbour,
        ).wait_send()
    holder = me // LEVELS
    here = holder == member
    for count in (LEVELS - 1, LEVELS):
        @pl.when(here == (count < LEVELS))
        def _():
            remote(
                context.at[1, pl.ds(0, count)], context.at[0, pl.ds(0, count)],
                context_send, context_recv, neighbour,
            ).wait_send()

    @pl.when(jnp.logical_and(jnp.logical_not(has_above), holder != me))
    def _():
        remote(source.at[0], source.at[1], source_send, source_recv, neighbour).wait_send()

    for side, goes in ((0, has_below), (1, has_above)):
        @pl.when(goes)
        def _():
            remote(
                edge_sent.at[side], edge_got.at[side], edge_send.at[side], edge_recv.at[side], neighbour
            ).wait_send()

    for store in stores:
        store.wait()


def solution(mesh):
    consts = constants()
    plane = jax.ShapeDtypeStruct((LEVELS, ROWS, N), jnp.float32)
    anywhere = pl.BlockSpec(memory_space=pl.ANY)
    smem = pl.BlockSpec(memory_space=pltpu.SMEM)
    f32 = jnp.float32

    def step(*args):
        return pl.pallas_call(
            kernel,
            out_shape=[plane] * 4,
            in_specs=[anywhere] * 5 + [smem] + [anywhere] * 7,
            out_specs=[anywhere] * 4,
            scratch_shapes=[
                pltpu.VMEM((2, LEVELS, 2, ROWS, N), f32),
                pltpu.VMEM((LEVELS, ROWS, N), f32),
                pltpu.VMEM((1 + LEVELS, 2, ROWS, N), f32),
                *[pltpu.VMEM(c.shape, c.dtype) for c in consts],
                pltpu.VMEM((2, N, LANES), f32),
                pltpu.VMEM((2, LEVELS, 3, ROWS, N), f32),
                pltpu.VMEM((2, 2, LEVELS, 2, ROWS, N), f32),
                pltpu.VMEM((TICKS, GROUP, LEVELS, ROWS, LANES), f32),
                pltpu.VMEM((TICKS, LAT, ROWS, LANES), f32),
                pltpu.VMEM((TICKS, LAT, ROWS, LANES), f32),
                pltpu.VMEM((TICKS - 1, 2, LAT // 2, ROWS, LANES), f32),
                pltpu.VMEM((LAT + 2 * GROUP, ROWS, LANES), f32),
                pltpu.VMEM((LEVELS, GROUP, ROWS, LANES), f32),
                *[pltpu.VMEM((2, ROWS, N), f32)] * 2,
                pltpu.SemaphoreType.DMA((12,)),
                pltpu.SemaphoreType.DMA((4,)),
                *[pltpu.SemaphoreType.DMA((TICKS,))] * 2,
                *[pltpu.SemaphoreType.DMA((TICKS - 1, 2))] * 2,
                *[pltpu.SemaphoreType.DMA((3,))] * 2,
                *[pltpu.SemaphoreType.DMA((2,))] * 2,
                *[pltpu.SemaphoreType.DMA] * 4,
            ],
            compiler_params=pltpu.CompilerParams(collective_id=0, has_side_effects=True),
        )(*args, *[jnp.asarray(c) for c in consts])

    lateral = P("depth", "lat", None)
    return jax.shard_map(
        step,
        mesh=mesh,
        in_specs=(lateral,) * 5 + (P("depth"), lateral, P("lat", None), P("lat", None)),
        out_specs=(lateral,) * 4,
        check_vma=False,
    )
```

time: 77 us -> 51.5 us (0.67)
  Pallas kernels: 62.7 us -> 47 us
  local copies, waits for them, and re-layouts: 12.8 us -> 3.54 us
    pallas_call x1, Pallas kernels: 62.7 us -> 47 us  [step(): pl.pallas_call(kernel, out_shape=[plane] * 4, in_specs=[anywhere] * 5 + [...]
    unnamed x30 -> x10, local copies, waits for them, and re-layouts: 12.8 us -> 3.54 us
where the time goes in v1:
time: 51.5 us; the launch traced here: 51.2 us
  Pallas kernels  47 us (91%)
  local copies, waits for them, and re-layouts  3.54 us (7%)
  between operations  0.65 us (1%)
    pallas_call x1, Pallas kernels, step(): pl.pallas_call(kernel, out_shape=[plane] * 4, in_specs=[anywhere] * 5 + [...  47 us
    unnamed x10, local copies, waits for them, and re-layouts  3.54 us

profile of v1, /device:TPU:1, one launch (start us, length us, event | category | flops | bytes accessed | tf_op | source)
XLA Modules:
  0.0 51.2 jit_solution(6807019805814407155)
XLA Ops:
  0.6 47.0 %shard_map.156 = (f32[4,8,256]{2,1,0:T(8,128)}, f32[4,8,256]{2,1,0:T(8,128)}, f32[4,8,256]{2,1,0:T(8,128)}, f32[4,8,256]{2,1,0:T(8,128)}) custom-call(f32[4,8,256]{2,1,0:T(8,128)} %down_real.1, f32[4,8,256]{2,1,0:T(8,128)} %down_imag.1, f32[4,8,256]{2,1,0:T(8,128)} %up_real.1, f32[4,8,256]{2,1,0:T(8,128)} %up_imag.1, f32[4,8,256]{2,1,0:T(8,128)} %slowness.1, ...), custom_call_target="tpu_custom_call" | custom-call | tf_op jit(solution)/shard_map/pallas_call | solution.py:610
  47.6 0.0 copy-start.2
  47.6 1.4 %copy.21 = f32[4,8,256]{2,1,0:T(8,128)} copy(f32[4,8,256]{2,1,0:T(8,128)} %get-tuple-element.8) | data formatting | bytes 65536
  49.0 0.0 copy-done.2
  49.0 0.0 copy-start.1
  49.0 0.6 %copy.22 = f32[4,8,256]{2,1,0:T(8,128)} copy(f32[4,8,256]{2,1,0:T(8,128)S(1)} %copy-done.2) | data formatting | bytes 65536
  49.6 0.2 copy-done.1
  49.8 0.0 copy-start
  49.8 0.6 %copy.23 = f32[4,8,256]{2,1,0:T(8,128)} copy(f32[4,8,256]{2,1,0:T(8,128)S(1)} %copy-done.1) | data formatting | bytes 65536
  50.4 0.2 copy-done
  50.6 0.6 %copy.24 = f32[4,8,256]{2,1,0:T(8,128)} copy(f32[4,8,256]{2,1,0:T(8,128)S(1)} %copy-done) | data formatting | bytes 65536
Async XLA Ops:
  47.6 1.4 %copy-start.2 = (f32[4,8,256]{2,1,0:T(8,128)S(1)}, f32[4,8,256]{2,1,0:T(8,128)}, u32[]{:S(2)}) copy-start(f32[4,8,256]{2,1,0:T(8,128)} %get-tuple-element.9) | copy-start | bytes 98308
  49.0 0.8 %copy-start.1 = (f32[4,8,256]{2,1,0:T(8,128)S(1)}, f32[4,8,256]{2,1,0:T(8,128)}, u32[]{:S(2)}) copy-start(f32[4,8,256]{2,1,0:T(8,128)} %get-tuple-element.10) | copy-start | bytes 98308
  49.8 0.8 %copy-start = (f32[4,8,256]{2,1,0:T(8,128)S(1)}, f32[4,8,256]{2,1,0:T(8,128)}, u32[]{:S(2)}) copy-start(f32[4,8,256]{2,1,0:T(8,128)} %get-tuple-element.11) | copy-start | bytes 98308

commit v2 on v1

--- a/solution.py
+++ b/solution.py
@@ -16,11 +16,12 @@
 LEVELS = 4
 GROUP = 8
 LAT = 32
+FAR = 20
 ROWS = 8
 N = 256
 LANES = 128
 HALF = 64
-SLOT = 16
+WAVES = N // GROUP
 
 
 def split(x):
@@ -38,32 +39,10 @@
 
 def constants():
     index = np.arange(N)
-    slot, device, row = np.meshgrid(np.arange(LEVELS), np.arange(GROUP), np.arange(ROWS), indexing="ij")
-    waves = (LAT * device + ROWS * slot + row).reshape(-1)
-    angle = 2.0 * np.pi * (np.outer(waves, index) % N) / N
+    angle = 2.0 * np.pi * (np.outer(index, index) % N) / N
     cos_hi, cos_lo = np_split(np.cos(angle))
     sin_hi, sin_lo = np_split(np.sin(angle))
-    full = np.stack([cos_hi, sin_hi, cos_lo, sin_lo])
-    coarse = np.arange(LAT)
-    angle = 2.0 * np.pi * (np.outer(coarse, coarse) % LAT) / LAT
-    eye = np.eye(ROWS)
-    both = np.concatenate([np.kron(np.cos(angle), eye), np.kron(np.sin(angle), eye)])
-    outer = np.stack(np_split(both))
-    fine = np.arange(ROWS)
-    angle = 2.0 * np.pi * (np.outer(fine, fine) % ROWS) / ROWS
-    cosine, sine = (np.kron(np.eye(HALF // ROWS), f(angle)) for f in (np.cos, np.sin))
-    inner = []
-    for sign in (1.0, -1.0):
-        block = np.block([[cosine, -sign * sine], [sign * sine, cosine]])
-        high, low = np_split(block)
-        inner.append(np.block([[high, low], [high, low]]))
-    inner = np.stack(inner)
-    turn = 2.0 * np.pi * np.outer(coarse, fine) / N
-    cosine = np.tile(np.cos(turn), (1, LANES // ROWS))
-    sine = np.tile(np.sin(turn), (1, LANES // ROWS))
-    sine[:, HALF:] *= -1.0
-    twiddle = np.stack([cosine, sine]).astype(np.float32)[:, :, None, :]
-    return full, outer, inner, twiddle
+    return np.stack([cos_hi, sin_hi, cos_lo, sin_lo])
 
 
 def dot(a, b, dims=((1,), (0,))):
@@ -74,13 +53,13 @@
     return lax.broadcasted_iota(jnp.int32, shape, len(shape) - 1)
 
 
-def slot_swap(tiles, roll):
-    slot = (lanes(tiles[0].shape) // SLOT) % LEVELS
+def block_swap(tiles, roll):
+    block = lanes(tiles[0].shape) // WAVES
     for bit in (2, 1):
-        keep = (slot & bit) == 0
-        shift = bit * SLOT
+        keep = (block & bit) == 0
+        shift = bit * WAVES
         new = list(tiles)
-        for a in range(LEVELS):
+        for a in range(4):
             if a & bit == 0:
                 low, high = tiles[a], tiles[a + bit]
                 new[a] = jnp.where(keep, low, roll(high, shift))
@@ -89,71 +68,65 @@
     return tiles
 
 
-def forward_y(real, imag, full, roll):
+def along_y(real, imag, full, sign):
     real_hi, real_lo = split(real)
     imag_hi, imag_lo = split(imag)
-    same = jnp.concatenate([real_hi, imag_hi, real_lo, imag_lo], axis=0)
-    swapped = jnp.concatenate([imag_hi, -real_hi, imag_lo, -real_lo], axis=0)
-    last = ((1,), (1,))
-    wide = dot(full[0], same, last) + dot(full[1], swapped, last)
-    rest = dot(full[2], same[:LANES], last) + dot(full[3], swapped[:LANES], last)
-    total = wide[:, :LANES] + (wide[:, LANES:] + rest)
-    return slot_swap([total[HALF * a : HALF * (a + 1)] for a in range(LEVELS)], roll)
+    both = jnp.concatenate([real_hi, imag_hi, real_lo, imag_lo], axis=0)
+    cosine = dot(both, full[0])
+    sine = dot(both, full[1])
+    cosine = cosine[:LANES] + (cosine[LANES:] + dot(both[:LANES], full[2]))
+    sine = sine[:LANES] + (sine[LANES:] + dot(both[:LANES], full[3]))
+    if sign < 0:
+        return cosine[:HALF] + sine[HALF:], cosine[HALF:] - sine[:HALF]
+    return cosine[:HALF] - sine[HALF:], cosine[HALF:] + sine[:HALF]
+
+
+def to_tiles(real, imag, roll):
+    parts = [x.reshape(LEVELS, 2, ROWS, N) for x in (real, imag)]
+    rows = [parts[c][:, du] for c in range(2) for du in range(2)]
+    halves = [block_swap([x[:, :, LANES * h : LANES * (h + 1)] for x in rows], roll) for h in range(2)]
+    return jnp.stack([halves[h][b] for h in range(2) for b in range(4)])
+
+
+def from_tiles(tiles, roll):
+    halves = [block_swap([tiles[:, 4 * h + b] for b in range(4)], roll) for h in range(2)]
+    rows = [jnp.concatenate([halves[0][b], halves[1][b]], axis=-1) for b in range(4)]
+    return (
+        jnp.stack([rows[0], rows[1]], axis=1).reshape(HALF, N),
+        jnp.stack([rows[2], rows[3]], axis=1).reshape(HALF, N),
+    )
 
 
 def signs(shape):
     return jnp.where(lanes(shape) < HALF, 1.0, -1.0).astype(jnp.float32)
 
 
-def outer_step(x, outer, sign, roll):
+def along_x(x, full, sign, roll):
     high, low = split(x)
-    wide = dot(outer[0], jnp.concatenate([high, low], axis=1))
-    total = wide[:, :LANES] + (wide[:, LANES:] + dot(outer[1], high))
+    wide = dot(full[0:2].reshape(2 * N, N), jnp.concatenate([high, low], axis=1))
+    rest = dot(full[2:4].reshape(2 * N, N), high)
+    total = wide[:, :LANES] + (wide[:, LANES:] + rest)
     return total[:N] + sign * roll(total[N:], HALF)
-
-
-def inner_step(x, inner):
-    high, low = split(x)
-    wide = dot(jnp.concatenate([high, low], axis=1), inner)
-    return wide[:, :LANES] + wide[:, LANES:]
 
 
 def turned(x, cosine, sine, roll):
     return x * cosine + roll(x, HALF) * sine
 
 
-def middle(x, mult_real, mult_imag, outer, inner, twiddle, roll):
+def middle(x, mult_real, mult_imag, full, roll):
     sign = signs((N, LANES))
-    shape = (LAT, ROWS, LANES)
-    cosine = jnp.broadcast_to(twiddle[0], shape).reshape(N, LANES)
-    sine = jnp.broadcast_to(twiddle[1], shape).reshape(N, LANES)
-    x = outer_step(x, outer, sign, roll)
-    x = turned(x, cosine, sine, roll)
-    x = inner_step(x, inner[0])
+    x = along_x(x, full, sign, roll)
     x = turned(x, mult_real, mult_imag, roll)
-    x = inner_step(x, inner[1])
-    x = turned(x, cosine, -sine, roll)
-    return outer_step(x, outer, -sign, roll)
+    return along_x(x, full, -sign, roll)
 
 
 def is_down(shape):
-    return (lanes(shape) // ROWS) % 2 == 0
+    return (lanes(shape) // WAVES) % 2 == 0
 
 
 def packed(even, odd, roll):
     down = is_down(even.shape)
-    return jnp.where(down, even, roll(odd, ROWS)), jnp.where(down, roll(even, LANES - ROWS), odd)
-
-
-def backward_y(tiles, full, roll):
-    x = jnp.concatenate(slot_swap(tiles, roll), axis=0)
-    high, low = split(x.T)
-    both = jnp.concatenate([high, low], axis=0)
-    cosine = dot(both, full[0])
-    sine = dot(both, full[1])
-    cosine = cosine[:LANES] + (cosine[LANES:] + dot(high, full[2]))
-    sine = sine[:LANES] + (sine[LANES:] + dot(high, full[3]))
-    return cosine[:HALF] - sine[HALF:], cosine[HALF:] + sine[:HALF]
+    return jnp.where(down, even, roll(odd, WAVES)), jnp.where(down, roll(even, LANES - WAVES), odd)
 
 
 def wrapped_numbers(index):
@@ -164,8 +137,8 @@
 def multiplier(member, slow):
     row = lax.broadcasted_iota(jnp.int32, (N, LANES), 0)
     lane = lax.broadcasted_iota(jnp.int32, (N, LANES), 1)
-    wave_x = wrapped_numbers(row // ROWS + LAT * (lane % ROWS))
-    wave_y = wrapped_numbers(LAT * member + ROWS * ((lane // SLOT) % LEVELS) + row % ROWS)
+    wave_x = wrapped_numbers(row)
+    wave_y = wrapped_numbers(WAVES * member + lane % WAVES)
     argument = (OMEGA * slow) ** 2 - (wave_x * wave_x + wave_y * wave_y)
     vertical = jnp.sqrt(jnp.maximum(argument, 0.0))
     factor = jnp.exp(-jnp.sqrt(jnp.maximum(-argument, 0.0))) * (1.0 / (N * N))
@@ -187,9 +160,8 @@
 
 def kernel(
     down_real, down_imag, up_real, up_imag, slowness, ref_slow, reflect, source_real, source_imag,
-    full_hbm, outer_hbm, inner_hbm, twiddle_hbm,
-    out_dr, out_di, out_ur, out_ui,
-    state, slow, source, full, outer, inner, twiddle,
+    full_hbm, out_state,
+    state, slow, source, full,
     mult, context, corr, sent_there, got_there, sent_back, got_back, got_last, tiles, edge_sent, edge_got,
     in_sems, out_sems, there_send, there_recv, back_send, back_recv, last_send, last_recv,
     edge_send, edge_recv, context_send, context_recv, source_send, source_recv,
@@ -197,16 +169,21 @@
     me = lax.axis_index("lat")
     depth = lax.axis_index("depth")
     depths = lax.axis_size("depth")
-    member = lax.rem(me, GROUP)
-    column = me // GROUP
+    cell_x, cell_y, core = me // 8, lax.rem(me // 2, 4), lax.rem(me, 2)
+    member = 4 * lax.rem(cell_x, 2) + 2 * lax.rem(cell_y, 2) + core
+    block = jnp.where(cell_x >= 2, 3 - cell_y // 2, cell_y // 2)
     flipped = lax.rem(depth, 2)
-    level = jnp.where(flipped == 1, LEVELS - 1 - column, column)
+    level = jnp.where(flipped == 1, LEVELS - 1 - block, block)
     has_above = depth > 0
     has_below = depth < depths - 1
     last = TICKS - 1
 
-    def column_of(z):
+    def block_of(z):
         return jnp.where(flipped == 1, LEVELS - 1 - z, z)
+
+    def device_of(block, member):
+        block_x, block_y = block // 2, lax.rem(block + 1, 4) // 2
+        return 16 * block_x + 4 * block_y + 8 * (member // 4) + lax.rem(member, 4)
 
     def roll(x, shift):
         return pltpu.roll(x, shift, x.ndim - 1)
@@ -224,8 +201,7 @@
         for n, (src, dst) in enumerate([
             (down_real, state.at[0, :, 0]), (up_real, state.at[0, :, 1]),
             (down_imag, state.at[1, :, 0]), (up_imag, state.at[1, :, 1]),
-            (full_hbm, full), (outer_hbm, outer), (inner_hbm, inner), (twiddle_hbm, twiddle),
-            (slowness, slow), (reflect, context.at[1, :, 2]),
+            (full_hbm, full), (slowness, slow), (reflect, context.at[1, :, 2]),
             (source_real, source.at[0, 0]), (source_imag, source.at[0, 1]),
         ])
     ]
@@ -257,16 +233,20 @@
         pl.semaphore_wait(barrier, LAT - 1 + has_above.astype(jnp.int32) + has_below.astype(jnp.int32))
 
         def send(step, _):
-            peer = lax.bitwise_xor(me, step)
+            peer = lax.bitwise_xor(me, lax.bitwise_xor(step, FAR))
+            peer_x, peer_y = peer // 8, lax.rem(peer // 2, 4)
+            peer_block = jnp.where(peer_x >= 2, 3 - peer_y // 2, peer_y // 2)
+            peer_member = 4 * lax.rem(peer_x, 2) + 2 * lax.rem(peer_y, 2) + lax.rem(peer, 2)
             remote(
-                sent_there.at[0, lax.rem(peer, GROUP), column_of(peer // GROUP)],
+                sent_there.at[0, peer_member, block_of(peer_block)],
                 got_there.at[0, me], there_send.at[0], there_recv.at[0], (depth, peer),
             ).start()
             return 0
 
-        lax.fori_loop(1, LAT, send, 0)
+        lax.fori_loop(0, FAR, send, 0)
+        lax.fori_loop(FAR + 1, LAT, send, 0)
         got_there[0, me] = sent_there[0, member, level]
-        for load in loads[8:]:
+        for load in loads[5:]:
             load.wait()
         for z in range(LEVELS):
             slow[z] = OMEGA * (slow[z] - ref_slow[z])
@@ -289,8 +269,6 @@
         mine = ref_slow[0]
         for z in range(1, LEVELS):
             mine = jnp.where(level == z, ref_slow[z], mine)
-        for load in loads[5:8]:
-            load.wait()
         mult[0], mult[1] = multiplier(member, mine)
         nothing = jnp.zeros((ROWS, N), jnp.float32)
 
@@ -315,7 +293,7 @@
         holder = me // LEVELS
         place = lax.rem(me, LEVELS)
         for z in range(LEVELS):
-            target = column_of(z) * GROUP + holder
+            target = device_of(block_of(z), holder)
 
             @pl.when(target != me)
             def _():
@@ -329,55 +307,65 @@
 
         @pl.when(jnp.logical_not(has_above))
         def _():
-            @pl.when(holder != me)
+            target = device_of(0, holder)
+
+            @pl.when(target != me)
             def _():
                 remote(
-                    source.at[0], source.at[1 + place], source_send, source_recv, (depth, holder)
+                    source.at[0], source.at[1 + place], source_send, source_recv, (depth, target)
                 ).start()
 
-            @pl.when(holder == me)
+            @pl.when(target == me)
             def _():
                 source[1 + place] = source[0]
 
     def later_there(tick):
         def send(step, _):
-            peer = lax.bitwise_xor(member, step)
+            peer = lax.bitwise_xor(member, GROUP - step)
             remote(
                 sent_there.at[tick, peer], got_there.at[tick, pl.ds(LEVELS * member, LEVELS)],
-                there_send.at[tick], there_recv.at[tick], (depth, column * GROUP + peer),
+                there_send.at[tick], there_recv.at[tick], (depth, device_of(block, peer)),
             ).start()
             return 0
 
         lax.fori_loop(1, GROUP, send, 0)
         got_there[tick, pl.ds(LEVELS * member, LEVELS)] = sent_there[tick, member]
 
+    def far_member(to_block):
+        across = (to_block // 2) != (block // 2)
+        return jnp.where(to_block == block, 6, jnp.where(across, 2, 4))
+
     def group_back(tick):
-        forth = jnp.where(flipped == 1, -1, 1)
         is_last = level == LEVELS - 1
         is_first = level == 0
-        down_to = (
-            depth + is_last.astype(jnp.int32), (column + jnp.where(is_last, 0, forth)) * GROUP,
-        )
-        up_to = (
-            depth - is_first.astype(jnp.int32), (column - jnp.where(is_first, 0, forth)) * GROUP,
-        )
+        down_depth = depth + is_last.astype(jnp.int32)
+        up_depth = depth - is_first.astype(jnp.int32)
+        forth = jnp.where(flipped == 1, -1, 1)
+        down_block = block + jnp.where(is_last, 0, forth)
+        up_block = block - jnp.where(is_first, 0, forth)
         goes_down = jnp.logical_or(has_below, jnp.logical_not(is_last))
         goes_up = jnp.logical_or(has_above, jnp.logical_not(is_first))
-        sides = ((0, goes_down, down_to), (1, goes_up, up_to))
-        for side, goes, (to_depth, base) in sides:
-            @pl.when(goes)
-            def _():
-                def send(step, _):
-                    peer = lax.bitwise_xor(member, step)
+        sides = (
+            (0, goes_down, down_depth, down_block, far_member(down_block)),
+            (1, goes_up, up_depth, up_block, far_member(up_block)),
+        )
+
+        def send(step, _):
+            for side, goes, to_depth, to_block, far in sides:
+                @pl.when(goes)
+                def _():
+                    peer = lax.bitwise_xor(member, lax.bitwise_xor(step, far))
                     remote(
                         sent_back.at[tick, pl.ds(LAT // 2 * side + 2 * peer, 2)],
                         got_back.at[tick, side, pl.ds(2 * member, 2)],
-                        back_send.at[tick, side], back_recv.at[tick, side], (to_depth, base + peer),
+                        back_send.at[tick, side], back_recv.at[tick, side],
+                        (to_depth, device_of(to_block, peer)),
                     ).start()
-                    return 0
-
-                lax.fori_loop(0, GROUP, send, 0)
-        return sides
+
+            return 0
+
+        lax.fori_loop(0, GROUP, send, 0)
+        return goes_down, goes_up
 
     def group_back_waits(tick, side):
         return remote(
@@ -394,8 +382,8 @@
     def one_tick(tick, _):
         real = state[0].reshape(HALF, N)
         imag = state[1].reshape(HALF, N)
-        for g, x in enumerate(forward_y(real, imag, full, roll)):
-            sent_there[tick, :, g] = x.reshape(GROUP, ROWS, LANES)
+        real, imag = along_y(real, imag, full, -1)
+        sent_there[tick] = to_tiles(real, imag, roll)
 
         @pl.when(tick == 0)
         def _():
@@ -415,7 +403,7 @@
             ).wait_recv()
 
         x = got_there[tick].reshape(N, LANES)
-        x = middle(x, mult[0], mult[1], outer, inner, twiddle, roll).reshape(LAT, ROWS, LANES)
+        x = middle(x, mult[0], mult[1], full, roll).reshape(LAT, ROWS, LANES)
 
         @pl.when(tick < last)
         def _():
@@ -423,7 +411,7 @@
             down, up = packed(pairs[:, 0], pairs[:, 1], roll)
             sent_back[tick, : LAT // 2] = down
             sent_back[tick, LAT // 2 :] = up
-            sides = group_back(tick)
+            goes = group_back(tick)
 
             def fill(which):
                 angle = context[which, :, 0:2]
@@ -432,8 +420,7 @@
 
             @pl.when(tick == 0)
             def _():
-                holder = member * LEVELS
-                here = jnp.logical_and(me >= holder, me < holder + LEVELS)
+                here = me // LEVELS == member
                 for count in (LEVELS - 1, LEVELS):
                     @pl.when(here == (count < LEVELS))
                     def _():
@@ -442,7 +429,7 @@
                             context_send, context_recv, neighbour,
                         ).wait_recv()
 
-                    @pl.when(jnp.logical_and(jnp.logical_not(has_above), column == 0))
+                    @pl.when(jnp.logical_and(jnp.logical_not(has_above), block == 0))
                     def _():
                         @pl.when(here == (count < LEVELS))
                         def _():
@@ -472,8 +459,8 @@
             up = got_back[tick, 1].reshape(GROUP, 2, ROWS, LANES)
             for j in range(2):
                 tiles[2 * j], tiles[2 * j + 1] = packed(down[:, j], up[:, j], roll)
-            for side, goes, _ in sides:
-                @pl.when(goes)
+            for side in range(2):
+                @pl.when(goes[side])
                 def _():
                     group_back_waits(tick, side).wait_send()
 
@@ -483,7 +470,7 @@
             slot = level * GROUP + member
 
             def send(step, _):
-                peer = lax.bitwise_xor(me, step)
+                peer = lax.bitwise_xor(me, lax.bitwise_xor(step, FAR))
                 remote(
                     sent_back.at[last, peer], got_last.at[slot],
                     last_send.at[0], last_recv.at[0], (depth, peer),
@@ -492,7 +479,7 @@
 
             def send_past(side, where, place):
                 def send(step, _):
-                    peer = lax.bitwise_xor(me, step)
+                    peer = lax.bitwise_xor(me, lax.bitwise_xor(step, FAR))
                     remote(
                         sent_back.at[last, peer], got_last.at[place + member],
                         last_send.at[side], last_recv.at[side], (where, peer),
@@ -512,7 +499,8 @@
             def _():
                 send_past(2, depth - 1, LAT + GROUP)
 
-            lax.fori_loop(1, LAT, send, 0)
+            lax.fori_loop(0, FAR, send, 0)
+            lax.fori_loop(FAR + 1, LAT, send, 0)
             got_last[slot] = sent_back[last, me]
             for side, comes, place in ((1, has_above, LAT), (2, has_below, LAT + GROUP)):
                 @pl.when(comes)
@@ -537,7 +525,7 @@
                 def _():
                     last_waits(side, LAT, 0).wait_send()
 
-        real, imag = backward_y([tiles[g].reshape(HALF, LANES) for g in range(LEVELS)], full, roll)
+        real, imag = along_y(*from_tiles(tiles[...], roll), full, 1)
         real = real.reshape(LEVELS, 2, ROWS, N)
         imag = imag.reshape(LEVELS, 2, ROWS, N)
         at_end = (tick == last).astype(jnp.int32)
@@ -555,15 +543,8 @@
         return 0
 
     lax.fori_loop(0, TICKS, one_tick, 0)
-    stores = [
-        pltpu.make_async_copy(src, dst, out_sems.at[n])
-        for n, (src, dst) in enumerate([
-            (state.at[0, :, 0], out_dr), (state.at[1, :, 0], out_di),
-            (state.at[0, :, 1], out_ur), (state.at[1, :, 1], out_ui),
-        ])
-    ]
-    for store in stores:
-        store.start()
+    store = pltpu.make_async_copy(state, out_state, out_sems.at[0])
+    store.start()
 
     remote(
         got_there.at[0, pl.ds(0, LAT - 1)], got_there.at[0, pl.ds(0, LAT - 1)],
@@ -584,7 +565,7 @@
                 context_send, context_recv, neighbour,
             ).wait_send()
 
-    @pl.when(jnp.logical_and(jnp.logical_not(has_above), holder != me))
+    @pl.when(jnp.logical_and(jnp.logical_not(has_above), device_of(0, holder) != me))
     def _():
         remote(source.at[0], source.at[1], source_send, source_recv, neighbour).wait_send()
 
@@ -595,28 +576,35 @@
                 edge_sent.at[side], edge_got.at[side], edge_send.at[side], edge_recv.at[side], neighbour
             ).wait_send()
 
-    for store in stores:
-        store.wait()
+    store.wait()
+
+
+def handed_out(state, out_dr, out_di, out_ur, out_ui):
+    out_dr[...] = state[0, :, 0]
+    out_di[...] = state[1, :, 0]
+    out_ur[...] = state[0, :, 1]
+    out_ui[...] = state[1, :, 1]
 
 
 def solution(mesh):
-    consts = constants()
+    full = constants()
     plane = jax.ShapeDtypeStruct((LEVELS, ROWS, N), jnp.float32)
     anywhere = pl.BlockSpec(memory_space=pl.ANY)
     smem = pl.BlockSpec(memory_space=pltpu.SMEM)
+    whole = pl.BlockSpec(memory_space=pltpu.VMEM)
     f32 = jnp.float32
 
     def step(*args):
-        return pl.pallas_call(
+        state = pl.pallas_call(
             kernel,
-            out_shape=[plane] * 4,
-            in_specs=[anywhere] * 5 + [smem] + [anywhere] * 7,
-            out_specs=[anywhere] * 4,
+            out_shape=jax.ShapeDtypeStruct((2, LEVELS, 2, ROWS, N), f32),
+            in_specs=[anywhere] * 5 + [smem] + [anywhere] * 4,
+            out_specs=anywhere,
             scratch_shapes=[
                 pltpu.VMEM((2, LEVELS, 2, ROWS, N), f32),
                 pltpu.VMEM((LEVELS, ROWS, N), f32),
                 pltpu.VMEM((1 + LEVELS, 2, ROWS, N), f32),
-                *[pltpu.VMEM(c.shape, c.dtype) for c in consts],
+                pltpu.VMEM(full.shape, jnp.bfloat16),
                 pltpu.VMEM((2, N, LANES), f32),
                 pltpu.VMEM((2, LEVELS, 3, ROWS, N), f32),
                 pltpu.VMEM((2, 2, LEVELS, 2, ROWS, N), f32),
@@ -627,8 +615,8 @@
                 pltpu.VMEM((LAT + 2 * GROUP, ROWS, LANES), f32),
                 pltpu.VMEM((LEVELS, GROUP, ROWS, LANES), f32),
                 *[pltpu.VMEM((2, ROWS, N), f32)] * 2,
-                pltpu.SemaphoreType.DMA((12,)),
-                pltpu.SemaphoreType.DMA((4,)),
+                pltpu.SemaphoreType.DMA((9,)),
+                pltpu.SemaphoreType.DMA((1,)),
                 *[pltpu.SemaphoreType.DMA((TICKS,))] * 2,
                 *[pltpu.SemaphoreType.DMA((TICKS - 1, 2))] * 2,
                 *[pltpu.SemaphoreType.DMA((3,))] * 2,
@@ -636,7 +624,13 @@
                 *[pltpu.SemaphoreType.DMA] * 4,
             ],
             compiler_params=pltpu.CompilerParams(collective_id=0, has_side_effects=True),
-        )(*args, *[jnp.asarray(c) for c in consts])
+        )(*args, jnp.asarray(full))
+        return pl.pallas_call(
+            handed_out,
+            out_shape=[plane] * 4,
+            in_specs=[whole],
+            out_specs=[whole] * 4,
+        )(state)
 
     lateral = P("depth", "lat", None)
     return jax.shard_map(

time: 51.5 us -> 45.3 us (0.88)
  local copies, waits for them, and re-layouts: 3.54 us -> 0 us
  Pallas kernels: 47 us -> 44.5 us
    unnamed x10 -> x0, local copies, waits for them, and re-layouts: 3.54 us -> none
    pallas_call x1 -> x2, Pallas kernels: 47 us -> 44.5 us  [the longest x1 43 us: step(): pl.pallas_call(kernel, out_shape=jax.ShapeDtypeStruct((2, LEVELS, 2, ROWS...]
where the time goes in v2:
time: 45.3 us; the launch traced here: 45.2 us
  Pallas kernels  44.5 us (98%)
  between operations  0.64 us (1%)
    pallas_call x1, Pallas kernels, step(): pl.pallas_call(kernel, out_shape=jax.ShapeDtypeStruct((2, LEVELS, 2, ROWS...  43 us
    pallas_call x1, Pallas kernels, step(): pl.pallas_call(handed_out, out_shape=[plane] * 4, in_specs=[whole], out_s...  1.56 us

profile of v2, /device:TPU:1, one launch (start us, length us, event | category | flops | bytes accessed | tf_op | source)
XLA Modules:
  0.0 45.2 jit_solution(3021206402258840325)
XLA Ops:
  0.6 43.0 %shard_map.129.state = f32[2,4,2,8,256]{4,3,2,1,0:T(8,128)} custom-call(f32[4,8,256]{2,1,0:T(8,128)} %down_real.1, f32[4,8,256]{2,1,0:T(8,128)} %down_imag.1, f32[4,8,256]{2,1,0:T(8,128)} %up_real.1, f32[4,8,256]{2,1,0:T(8,128)} %up_imag.1, f32[4,8,256]{2,1,0:T(8,128)} %slowness.1, f32[4]{0:T(128)} %ref_slow.1, f32[4,8,256]{2,1,0:T(8,128)} %reflect.1, ...), custom_call_target="tpu_custom_call" | custom-call | tf_op jit(solution)/shard_map/pallas_call | solution.py:598
  43.6 1.6 %shard_map.130 = (f32[4,8,256]{2,1,0:T(8,128)}, f32[4,8,256]{2,1,0:T(8,128)}, f32[4,8,256]{2,1,0:T(8,128)}, f32[4,8,256]{2,1,0:T(8,128)}) custom-call(f32[2,4,2,8,256]{4,3,2,1,0:T(8,128)} %shard_map.129.state), custom_call_target="tpu_custom_call" | custom-call | tf_op jit(solution)/shard_map/pallas_call | solution.py:628

commit v3 on v2

--- a/solution.py
+++ b/solution.py
@@ -88,13 +88,14 @@
     return jnp.stack([halves[h][b] for h in range(2) for b in range(4)])
 
 
-def from_tiles(tiles, roll):
-    halves = [block_swap([tiles[:, 4 * h + b] for b in range(4)], roll) for h in range(2)]
-    rows = [jnp.concatenate([halves[0][b], halves[1][b]], axis=-1) for b in range(4)]
-    return (
-        jnp.stack([rows[0], rows[1]], axis=1).reshape(HALF, N),
-        jnp.stack([rows[2], rows[3]], axis=1).reshape(HALF, N),
-    )
+def from_tiles(x, roll):
+    halves = [block_swap([x[4 * h + a] for a in range(4)], roll) for h in range(2)]
+    return [jnp.concatenate([halves[0][b], halves[1][b]], axis=-1) for b in range(4)]
+
+
+def from_pairs(x, roll):
+    rows = [from_tiles(x[:, j], roll) for j in range(2)]
+    return [jnp.stack([rows[g // 2][2 * part + g % 2] for g in range(LEVELS)]) for part in range(2)]
 
 
 def signs(shape):
@@ -160,10 +161,10 @@
 
 def kernel(
     down_real, down_imag, up_real, up_imag, slowness, ref_slow, reflect, source_real, source_imag,
-    full_hbm, out_state,
-    state, slow, source, full,
-    mult, context, corr, sent_there, got_there, sent_back, got_back, got_last, tiles, edge_sent, edge_got,
-    in_sems, out_sems, there_send, there_recv, back_send, back_recv, last_send, last_recv,
+    full_hbm, state,
+    slow, source, full,
+    mult, context, corr, sent_there, got_there, sent_back, got_back, got_last, edge_sent, edge_got,
+    in_sems, there_send, there_recv, back_send, back_recv, last_send, last_recv,
     edge_send, edge_recv, context_send, context_recv, source_send, source_recv,
 ):
     me = lax.axis_index("lat")
@@ -211,12 +212,12 @@
     barrier = pltpu.get_barrier_semaphore()
 
     def greet(step, _):
-        pl.semaphore_signal(
-            barrier, inc=1, device_id=(depth, lax.bitwise_xor(me, step)), device_id_type=MESH
-        )
+        peer = lax.bitwise_xor(me, lax.bitwise_xor(step, FAR))
+        pl.semaphore_signal(barrier, inc=1, device_id=(depth, peer), device_id_type=MESH)
         return 0
 
-    lax.fori_loop(1, LAT, greet, 0)
+    lax.fori_loop(0, FAR, greet, 0)
+    lax.fori_loop(FAR + 1, LAT, greet, 0)
 
     @pl.when(has_above)
     def _():
@@ -457,8 +458,9 @@
 
             down = got_back[tick, 0].reshape(GROUP, 2, ROWS, LANES)
             up = got_back[tick, 1].reshape(GROUP, 2, ROWS, LANES)
-            for j in range(2):
-                tiles[2 * j], tiles[2 * j + 1] = packed(down[:, j], up[:, j], roll)
+            for du, got in enumerate((down, up)):
+                for part, rows in enumerate(from_pairs(got, roll)):
+                    state[part, :, du] = rows
             for side in range(2):
                 @pl.when(goes[side])
                 def _():
@@ -469,38 +471,33 @@
             sent_back[last] = x
             slot = level * GROUP + member
 
+            goes_down = jnp.logical_and(level == LEVELS - 1, has_below)
+            goes_up = jnp.logical_and(level == 0, has_above)
+
             def send(step, _):
                 peer = lax.bitwise_xor(me, lax.bitwise_xor(step, FAR))
-                remote(
-                    sent_back.at[last, peer], got_last.at[slot],
-                    last_send.at[0], last_recv.at[0], (depth, peer),
-                ).start()
-                return 0
-
-            def send_past(side, where, place):
-                def send(step, _):
-                    peer = lax.bitwise_xor(me, lax.bitwise_xor(step, FAR))
+
+                def push(side, where, place):
                     remote(
-                        sent_back.at[last, peer], got_last.at[place + member],
+                        sent_back.at[last, peer], got_last.at[place],
                         last_send.at[side], last_recv.at[side], (where, peer),
                     ).start()
-                    return 0
-
-                lax.fori_loop(0, LAT, send, 0)
-
-            goes_down = jnp.logical_and(level == LEVELS - 1, has_below)
-            goes_up = jnp.logical_and(level == 0, has_above)
-
-            @pl.when(goes_down)
-            def _():
-                send_past(1, depth + 1, LAT)
-
-            @pl.when(goes_up)
-            def _():
-                send_past(2, depth - 1, LAT + GROUP)
-
-            lax.fori_loop(0, FAR, send, 0)
-            lax.fori_loop(FAR + 1, LAT, send, 0)
+
+                @pl.when(goes_down)
+                def _():
+                    push(1, depth + 1, LAT + member)
+
+                @pl.when(goes_up)
+                def _():
+                    push(2, depth - 1, LAT + GROUP + member)
+
+                @pl.when(peer != me)
+                def _():
+                    push(0, depth, slot)
+
+                return 0
+
+            lax.fori_loop(0, LAT, send, 0)
             got_last[slot] = sent_back[last, me]
             for side, comes, place in ((1, has_above, LAT), (2, has_below, LAT + GROUP)):
                 @pl.when(comes)
@@ -516,16 +513,16 @@
             for z in range(LEVELS):
                 above = GROUP * (z - 1) if z > 0 else LAT
                 below = GROUP * (z + 1) if z < LEVELS - 1 else LAT + GROUP
-                tiles[z] = jnp.where(
-                    down, got_last[above : above + GROUP], got_last[below : below + GROUP]
-                )
+                got = jnp.where(down, got_last[above : above + GROUP], got_last[below : below + GROUP])
+                for n, rows in enumerate(from_tiles(got, roll)):
+                    state[n // 2, z, n % 2] = rows
             last_waits(0, LAT - 1, 0).wait_send()
             for side, goes in ((1, goes_down), (2, goes_up)):
                 @pl.when(goes)
                 def _():
                     last_waits(side, LAT, 0).wait_send()
 
-        real, imag = along_y(*from_tiles(tiles[...], roll), full, 1)
+        real, imag = along_y(state[0].reshape(HALF, N), state[1].reshape(HALF, N), full, 1)
         real = real.reshape(LEVELS, 2, ROWS, N)
         imag = imag.reshape(LEVELS, 2, ROWS, N)
         at_end = (tick == last).astype(jnp.int32)
@@ -543,9 +540,6 @@
         return 0
 
     lax.fori_loop(0, TICKS, one_tick, 0)
-    store = pltpu.make_async_copy(state, out_state, out_sems.at[0])
-    store.start()
-
     remote(
         got_there.at[0, pl.ds(0, LAT - 1)], got_there.at[0, pl.ds(0, LAT - 1)],
         there_send.at[0], there_recv.at[0], neighbour,
@@ -576,14 +570,16 @@
                 edge_sent.at[side], edge_got.at[side], edge_send.at[side], edge_recv.at[side], neighbour
             ).wait_send()
 
-    store.wait()
-
-
-def handed_out(state, out_dr, out_di, out_ur, out_ui):
-    out_dr[...] = state[0, :, 0]
-    out_di[...] = state[1, :, 0]
-    out_ur[...] = state[0, :, 1]
-    out_ui[...] = state[1, :, 1]
+
+def handed_out(state, out_dr, out_di, out_ur, out_ui, sems):
+    copies = [
+        pltpu.make_async_copy(state.at[n % 2, :, n // 2], out, sems.at[n])
+        for n, out in enumerate((out_dr, out_di, out_ur, out_ui))
+    ]
+    for copy in copies:
+        copy.start()
+    for copy in copies:
+        copy.wait()
 
 
 def solution(mesh):
@@ -597,11 +593,10 @@
     def step(*args):
         state = pl.pallas_call(
             kernel,
-            out_shape=jax.ShapeDtypeStruct((2, LEVELS, 2, ROWS, N), f32),
+            out_shape=pltpu.VMEM((2, LEVELS, 2, ROWS, N), f32),
             in_specs=[anywhere] * 5 + [smem] + [anywhere] * 4,
-            out_specs=anywhere,
+            out_specs=whole,
             scratch_shapes=[
-                pltpu.VMEM((2, LEVELS, 2, ROWS, N), f32),
                 pltpu.VMEM((LEVELS, ROWS, N), f32),
                 pltpu.VMEM((1 + LEVELS, 2, ROWS, N), f32),
                 pltpu.VMEM(full.shape, jnp.bfloat16),
@@ -613,10 +608,8 @@
                 pltpu.VMEM((TICKS, LAT, ROWS, LANES), f32),
                 pltpu.VMEM((TICKS - 1, 2, LAT // 2, ROWS, LANES), f32),
                 pltpu.VMEM((LAT + 2 * GROUP, ROWS, LANES), f32),
-                pltpu.VMEM((LEVELS, GROUP, ROWS, LANES), f32),
                 *[pltpu.VMEM((2, ROWS, N), f32)] * 2,
                 pltpu.SemaphoreType.DMA((9,)),
-                pltpu.SemaphoreType.DMA((1,)),
                 *[pltpu.SemaphoreType.DMA((TICKS,))] * 2,
                 *[pltpu.SemaphoreType.DMA((TICKS - 1, 2))] * 2,
                 *[pltpu.SemaphoreType.DMA((3,))] * 2,
@@ -629,7 +622,9 @@
             handed_out,
             out_shape=[plane] * 4,
             in_specs=[whole],
-            out_specs=[whole] * 4,
+            out_specs=[anywhere] * 4,
+            scratch_shapes=[pltpu.SemaphoreType.DMA((4,))],
+            compiler_params=pltpu.CompilerParams(vmem_limit_bytes=2**20),
         )(state)
 
     lateral = P("depth", "lat", None)

time: 45.3 us -> 43.3 us (0.956)
  Pallas kernels: 44.5 us -> 42.5 us
    pallas_call x1, Pallas kernels: 43 us -> 41.8 us  [step(): pl.pallas_call(kernel, out_shape=pltpu.VMEM((2, LEVELS, 2, ROWS, N), f32)...]
    pallas_call x1, Pallas kernels: 1.56 us -> 0.68 us  [step(): pl.pallas_call(handed_out, out_shape=[plane] * 4, in_specs=[whole], out_s...]
where the time goes in v3:
time: 43.3 us; the launch traced here: 43.1 us
  Pallas kernels  42.5 us (98%)
  between operations  0.64 us (1%)
    pallas_call x1, Pallas kernels, step(): pl.pallas_call(kernel, out_shape=pltpu.VMEM((2, LEVELS, 2, ROWS, N), f32)...  41.8 us

profile of v3, /device:TPU:1, one launch (start us, length us, event | category | flops | bytes accessed | tf_op | source)
XLA Modules:
  0.0 43.1 jit_solution(13455901461408141786)
XLA Ops:
  0.6 41.8 %shard_map.129.state = f32[2,4,2,8,256]{4,3,2,1,0:T(8,128)S(1)} custom-call(f32[4,8,256]{2,1,0:T(8,128)} %down_real.1, f32[4,8,256]{2,1,0:T(8,128)} %down_imag.1, f32[4,8,256]{2,1,0:T(8,128)} %up_real.1, f32[4,8,256]{2,1,0:T(8,128)} %up_imag.1, f32[4,8,256]{2,1,0:T(8,128)} %slowness.1, f32[4]{0:T(128)} %ref_slow.1, f32[4,8,256]{2,1,0:T(8,128)} %reflect.1, ...), custom_call_target="tpu_custom_call" | custom-call | tf_op jit(solution)/shard_map/pallas_call | solution.py:594
  42.5 0.7 %shard_map.130 = (f32[4,8,256]{2,1,0:T(8,128)}, f32[4,8,256]{2,1,0:T(8,128)}, f32[4,8,256]{2,1,0:T(8,128)}, f32[4,8,256]{2,1,0:T(8,128)}) custom-call(f32[2,4,2,8,256]{4,3,2,1,0:T(8,128)S(1)} %shard_map.129.state), custom_call_target="tpu_custom_call" | custom-call | tf_op jit(solution)/shard_map/pallas_call | solution.py:621

commit v4 on v3

--- a/solution.py
+++ b/solution.py
@@ -21,6 +21,7 @@
 N = 256
 LANES = 128
 HALF = 64
+HALVES = N // 2
 WAVES = N // GROUP
 
 
@@ -38,11 +39,20 @@
 
 
 def constants():
-    index = np.arange(N)
-    angle = 2.0 * np.pi * (np.outer(index, index) % N) / N
-    cos_hi, cos_lo = np_split(np.cos(angle))
-    sin_hi, sin_lo = np_split(np.sin(angle))
-    return np.stack([cos_hi, sin_hi, cos_lo, sin_lo])
+    index = np.arange(HALVES)
+    angles = (
+        2.0 * np.pi * (np.outer(2 * index, index) % N) / N,
+        2.0 * np.pi * (np.outer(2 * index + 1, index) % N) / N,
+    )
+    even, odd = angles
+    by_row = []
+    for angle in (even, odd.T, odd):
+        for part in np_split(np.concatenate([np.cos(angle), np.sin(angle)], axis=1)):
+            by_row.append(np.concatenate([part, part], axis=0))
+    by_column = []
+    for angle in (even, odd, odd.T):
+        by_column.extend(np_split(np.concatenate([np.cos(angle), np.sin(angle)], axis=0)))
+    return np.stack(by_row), np.stack(by_column)
 
 
 def dot(a, b, dims=((1,), (0,))):
@@ -68,17 +78,26 @@
     return tiles
 
 
-def along_y(real, imag, full, sign):
-    real_hi, real_lo = split(real)
-    imag_hi, imag_lo = split(imag)
-    both = jnp.concatenate([real_hi, imag_hi, real_lo, imag_lo], axis=0)
-    cosine = dot(both, full[0])
-    sine = dot(both, full[1])
-    cosine = cosine[:LANES] + (cosine[LANES:] + dot(both[:LANES], full[2]))
-    sine = sine[:LANES] + (sine[LANES:] + dot(both[:LANES], full[3]))
+def along_y(real, imag, rows, sign):
+    x = jnp.concatenate([real, imag], axis=0)
+    first, second = x[:, :HALVES], x[:, HALVES:]
     if sign < 0:
-        return cosine[:HALF] + sine[HALF:], cosine[HALF:] - sine[:HALF]
-    return cosine[:HALF] - sine[HALF:], cosine[HALF:] + sine[:HALF]
+        first, second = first + second, first - second
+    out = []
+    for table, part in ((0, first), (2 if sign < 0 else 4, second)):
+        both = jnp.concatenate(split(part), axis=1)
+        total = dot(both, rows[table]) + dot(both, rows[table + 1])
+        cosine, sine = total[:, :HALVES], total[:, HALVES:]
+        if sign < 0:
+            out.append((cosine[:HALF] + sine[HALF:], cosine[HALF:] - sine[:HALF]))
+        else:
+            out.append((cosine[:HALF] - sine[HALF:], cosine[HALF:] + sine[:HALF]))
+    parts = []
+    for first, second in zip(*out):
+        if sign > 0:
+            first, second = first + second, first - second
+        parts.append(jnp.concatenate([first, second], axis=1))
+    return parts
 
 
 def to_tiles(real, imag, roll):
@@ -102,23 +121,31 @@
     return jnp.where(lanes(shape) < HALF, 1.0, -1.0).astype(jnp.float32)
 
 
-def along_x(x, full, sign, roll):
-    high, low = split(x)
-    wide = dot(full[0:2].reshape(2 * N, N), jnp.concatenate([high, low], axis=1))
-    rest = dot(full[2:4].reshape(2 * N, N), high)
-    total = wide[:, :LANES] + (wide[:, LANES:] + rest)
-    return total[:N] + sign * roll(total[N:], HALF)
+def along_x(x, columns, sign, roll):
+    first, second = x[:HALVES], x[HALVES:]
+    if sign < 0:
+        first, second = first + second, first - second
+    turn = -sign * signs((HALVES, LANES))
+    out = []
+    for table, part in ((0, first), (2 if sign < 0 else 4, second)):
+        high, low = split(part)
+        wide = dot(columns[table], jnp.concatenate([high, low], axis=1))
+        total = wide[:, :LANES] + (wide[:, LANES:] + dot(columns[table + 1], high))
+        out.append(total[:HALVES] + turn * roll(total[HALVES:], HALF))
+    first, second = out
+    if sign > 0:
+        first, second = first + second, first - second
+    return jnp.concatenate([first, second], axis=0)
 
 
 def turned(x, cosine, sine, roll):
     return x * cosine + roll(x, HALF) * sine
 
 
-def middle(x, mult_real, mult_imag, full, roll):
-    sign = signs((N, LANES))
-    x = along_x(x, full, sign, roll)
+def middle(x, mult_real, mult_imag, columns, roll):
+    x = along_x(x, columns, -1, roll)
     x = turned(x, mult_real, mult_imag, roll)
-    return along_x(x, full, -sign, roll)
+    return along_x(x, columns, 1, roll)
 
 
 def is_down(shape):
@@ -135,11 +162,15 @@
     return folded.astype(jnp.float32) * (2.0 * math.pi / N)
 
 
+def in_order(place):
+    return jnp.where(place < HALVES, 2 * place, 2 * (place - HALVES) + 1)
+
+
 def multiplier(member, slow):
     row = lax.broadcasted_iota(jnp.int32, (N, LANES), 0)
     lane = lax.broadcasted_iota(jnp.int32, (N, LANES), 1)
-    wave_x = wrapped_numbers(row)
-    wave_y = wrapped_numbers(WAVES * member + lane % WAVES)
+    wave_x = wrapped_numbers(in_order(row))
+    wave_y = wrapped_numbers(in_order(WAVES * member + lane % WAVES))
     argument = (OMEGA * slow) ** 2 - (wave_x * wave_x + wave_y * wave_y)
     vertical = jnp.sqrt(jnp.maximum(argument, 0.0))
     factor = jnp.exp(-jnp.sqrt(jnp.maximum(-argument, 0.0))) * (1.0 / (N * N))
@@ -161,8 +192,8 @@
 
 def kernel(
     down_real, down_imag, up_real, up_imag, slowness, ref_slow, reflect, source_real, source_imag,
-    full_hbm, state,
-    slow, source, full,
+    rows_hbm, columns_hbm, state,
+    slow, source, rows, columns,
     mult, context, corr, sent_there, got_there, sent_back, got_back, got_last, edge_sent, edge_got,
     in_sems, there_send, there_recv, back_send, back_recv, last_send, last_recv,
     edge_send, edge_recv, context_send, context_recv, source_send, source_recv,
@@ -202,8 +233,9 @@
         for n, (src, dst) in enumerate([
             (down_real, state.at[0, :, 0]), (up_real, state.at[0, :, 1]),
             (down_imag, state.at[1, :, 0]), (up_imag, state.at[1, :, 1]),
-            (full_hbm, full), (slowness, slow), (reflect, context.at[1, :, 2]),
+            (rows_hbm, rows), (slowness, slow), (reflect, context.at[1, :, 2]),
             (source_real, source.at[0, 0]), (source_imag, source.at[0, 1]),
+            (columns_hbm, columns),
         ])
     ]
     for load in loads:
@@ -383,7 +415,7 @@
     def one_tick(tick, _):
         real = state[0].reshape(HALF, N)
         imag = state[1].reshape(HALF, N)
-        real, imag = along_y(real, imag, full, -1)
+        real, imag = along_y(real, imag, rows, -1)
         sent_there[tick] = to_tiles(real, imag, roll)
 
         @pl.when(tick == 0)
@@ -404,7 +436,7 @@
             ).wait_recv()
 
         x = got_there[tick].reshape(N, LANES)
-        x = middle(x, mult[0], mult[1], full, roll).reshape(LAT, ROWS, LANES)
+        x = middle(x, mult[0], mult[1], columns, roll).reshape(LAT, ROWS, LANES)
 
         @pl.when(tick < last)
         def _():
@@ -459,8 +491,8 @@
             down = got_back[tick, 0].reshape(GROUP, 2, ROWS, LANES)
             up = got_back[tick, 1].reshape(GROUP, 2, ROWS, LANES)
             for du, got in enumerate((down, up)):
-                for part, rows in enumerate(from_pairs(got, roll)):
-                    state[part, :, du] = rows
+                for part, piece in enumerate(from_pairs(got, roll)):
+                    state[part, :, du] = piece
             for side in range(2):
                 @pl.when(goes[side])
                 def _():
@@ -514,15 +546,15 @@
                 above = GROUP * (z - 1) if z > 0 else LAT
                 below = GROUP * (z + 1) if z < LEVELS - 1 else LAT + GROUP
                 got = jnp.where(down, got_last[above : above + GROUP], got_last[below : below + GROUP])
-                for n, rows in enumerate(from_tiles(got, roll)):
-                    state[n // 2, z, n % 2] = rows
+                for n, piece in enumerate(from_tiles(got, roll)):
+                    state[n // 2, z, n % 2] = piece
             last_waits(0, LAT - 1, 0).wait_send()
             for side, goes in ((1, goes_down), (2, goes_up)):
                 @pl.when(goes)
                 def _():
                     last_waits(side, LAT, 0).wait_send()
 
-        real, imag = along_y(state[0].reshape(HALF, N), state[1].reshape(HALF, N), full, 1)
+        real, imag = along_y(state[0].reshape(HALF, N), state[1].reshape(HALF, N), rows, 1)
         real = real.reshape(LEVELS, 2, ROWS, N)
         imag = imag.reshape(LEVELS, 2, ROWS, N)
         at_end = (tick == last).astype(jnp.int32)
@@ -583,7 +615,7 @@
 
 
 def solution(mesh):
-    full = constants()
+    tables = constants()
     plane = jax.ShapeDtypeStruct((LEVELS, ROWS, N), jnp.float32)
     anywhere = pl.BlockSpec(memory_space=pl.ANY)
     smem = pl.BlockSpec(memory_space=pltpu.SMEM)
@@ -594,12 +626,12 @@
         state = pl.pallas_call(
             kernel,
             out_shape=pltpu.VMEM((2, LEVELS, 2, ROWS, N), f32),
-            in_specs=[anywhere] * 5 + [smem] + [anywhere] * 4,
+            in_specs=[anywhere] * 5 + [smem] + [anywhere] * 5,
             out_specs=whole,
             scratch_shapes=[
                 pltpu.VMEM((LEVELS, ROWS, N), f32),
                 pltpu.VMEM((1 + LEVELS, 2, ROWS, N), f32),
-                pltpu.VMEM(full.shape, jnp.bfloat16),
+                *[pltpu.VMEM(table.shape, jnp.bfloat16) for table in tables],
                 pltpu.VMEM((2, N, LANES), f32),
                 pltpu.VMEM((2, LEVELS, 3, ROWS, N), f32),
                 pltpu.VMEM((2, 2, LEVELS, 2, ROWS, N), f32),
@@ -609,7 +641,7 @@
                 pltpu.VMEM((TICKS - 1, 2, LAT // 2, ROWS, LANES), f32),
                 pltpu.VMEM((LAT + 2 * GROUP, ROWS, LANES), f32),
                 *[pltpu.VMEM((2, ROWS, N), f32)] * 2,
-                pltpu.SemaphoreType.DMA((9,)),
+                pltpu.SemaphoreType.DMA((10,)),
                 *[pltpu.SemaphoreType.DMA((TICKS,))] * 2,
                 *[pltpu.SemaphoreType.DMA((TICKS - 1, 2))] * 2,
                 *[pltpu.SemaphoreType.DMA((3,))] * 2,
@@ -617,7 +649,7 @@
                 *[pltpu.SemaphoreType.DMA] * 4,
             ],
             compiler_params=pltpu.CompilerParams(collective_id=0, has_side_effects=True),
-        )(*args, jnp.asarray(full))
+        )(*args, *[jnp.asarray(table) for table in tables])
         return pl.pallas_call(
             handed_out,
             out_shape=[plane] * 4,

time: 43.3 us -> 42.3 us (0.977)
  Pallas kernels: 42.5 us -> 41.5 us
    pallas_call x1, Pallas kernels: 41.8 us -> 40.8 us  [step(): pl.pallas_call(kernel, out_shape=pltpu.VMEM((2, LEVELS, 2, ROWS, N), f32)...]
where the time goes in v4:
time: 42.3 us; the launch traced here: 42.1 us
  Pallas kernels  41.5 us (98%)
  between operations  0.64 us (2%)
    pallas_call x1, Pallas kernels, step(): pl.pallas_call(kernel, out_shape=pltpu.VMEM((2, LEVELS, 2, ROWS, N), f32)...  40.8 us

profile of v4, /device:TPU:1, one launch (start us, length us, event | category | flops | bytes accessed | tf_op | source)
XLA Modules:
  0.0 42.1 jit_solution(1351466402305597018)
XLA Ops:
  0.6 40.8 %shard_map.138.state = f32[2,4,2,8,256]{4,3,2,1,0:T(8,128)S(1)} custom-call(f32[4,8,256]{2,1,0:T(8,128)} %down_real.1, f32[4,8,256]{2,1,0:T(8,128)} %down_imag.1, f32[4,8,256]{2,1,0:T(8,128)} %up_real.1, f32[4,8,256]{2,1,0:T(8,128)} %up_imag.1, f32[4,8,256]{2,1,0:T(8,128)} %slowness.1, f32[4]{0:T(128)} %ref_slow.1, f32[4,8,256]{2,1,0:T(8,128)} %reflect.1, ...), custom_call_target="tpu_custom_call" | custom-call | tf_op jit(solution)/shard_map/pallas_call | solution.py:626
  41.4 0.7 %shard_map.139 = (f32[4,8,256]{2,1,0:T(8,128)}, f32[4,8,256]{2,1,0:T(8,128)}, f32[4,8,256]{2,1,0:T(8,128)}, f32[4,8,256]{2,1,0:T(8,128)}) custom-call(f32[2,4,2,8,256]{4,3,2,1,0:T(8,128)S(1)} %shard_map.138.state), custom_call_target="tpu_custom_call" | custom-call | tf_op jit(solution)/shard_map/pallas_call | solution.py:653

commit v5 on v4

--- a/solution.py
+++ b/solution.py
@@ -238,9 +238,6 @@
             (columns_hbm, columns),
         ])
     ]
-    for load in loads:
-        load.start()
-
     barrier = pltpu.get_barrier_semaphore()
 
     def greet(step, _):
@@ -259,11 +256,33 @@
     def _():
         pl.semaphore_signal(barrier, inc=1, device_id=(depth + 1, me), device_id_type=MESH)
 
+    for load in loads:
+        load.start()
+
     for load in loads[:5]:
         load.wait()
 
     def first_there():
+        for load in loads[5:]:
+            load.wait()
+        for z in range(LEVELS):
+            slow[z] = OMEGA * (slow[z] - ref_slow[z])
+        edge_sent[0] = slow[LEVELS - 1]
+        edge_sent[1] = slow[0]
+        for z in range(LEVELS - 1):
+            context[1, z + 1, 0] = slow[z]
+            context[1, z, 1] = slow[z + 1]
         pl.semaphore_wait(barrier, LAT - 1 + has_above.astype(jnp.int32) + has_below.astype(jnp.int32))
+        down = remote(edge_sent.at[0], edge_got.at[0], edge_send.at[0], edge_recv.at[0], (depth + 1, me))
+        up = remote(edge_sent.at[1], edge_got.at[1], edge_send.at[1], edge_recv.at[1], (depth - 1, me))
+
+        @pl.when(has_below)
+        def _():
+            down.start()
+
+        @pl.when(has_above)
+        def _():
+            up.start()
 
         def send(step, _):
             peer = lax.bitwise_xor(me, lax.bitwise_xor(step, FAR))
@@ -279,26 +298,6 @@
         lax.fori_loop(0, FAR, send, 0)
         lax.fori_loop(FAR + 1, LAT, send, 0)
         got_there[0, me] = sent_there[0, member, level]
-        for load in loads[5:]:
-            load.wait()
-        for z in range(LEVELS):
-            slow[z] = OMEGA * (slow[z] - ref_slow[z])
-        edge_sent[0] = slow[LEVELS - 1]
-        edge_sent[1] = slow[0]
-        down = remote(edge_sent.at[0], edge_got.at[0], edge_send.at[0], edge_recv.at[0], (depth + 1, me))
-        up = remote(edge_sent.at[1], edge_got.at[1], edge_send.at[1], edge_recv.at[1], (depth - 1, me))
-
-        @pl.when(has_below)
-        def _():
-            down.start()
-
-        @pl.when(has_above)
-        def _():
-            up.start()
-
-        for z in range(LEVELS - 1):
-            context[1, z + 1, 0] = slow[z]
-            context[1, z, 1] = slow[z + 1]
         mine = ref_slow[0]
         for z in range(1, LEVELS):
             mine = jnp.where(level == z, ref_slow[z], mine)
@@ -398,7 +397,6 @@
             return 0
 
         lax.fori_loop(0, GROUP, send, 0)
-        return goes_down, goes_up
 
     def group_back_waits(tick, side):
         return remote(
@@ -444,7 +442,7 @@
             down, up = packed(pairs[:, 0], pairs[:, 1], roll)
             sent_back[tick, : LAT // 2] = down
             sent_back[tick, LAT // 2 :] = up
-            goes = group_back(tick)
+            group_back(tick)
 
             def fill(which):
                 angle = context[which, :, 0:2]
@@ -493,10 +491,6 @@
             for du, got in enumerate((down, up)):
                 for part, piece in enumerate(from_pairs(got, roll)):
                     state[part, :, du] = piece
-            for side in range(2):
-                @pl.when(goes[side])
-                def _():
-                    group_back_waits(tick, side).wait_send()
 
         @pl.when(tick == last)
         def _():
@@ -548,11 +542,6 @@
                 got = jnp.where(down, got_last[above : above + GROUP], got_last[below : below + GROUP])
                 for n, piece in enumerate(from_tiles(got, roll)):
                     state[n // 2, z, n % 2] = piece
-            last_waits(0, LAT - 1, 0).wait_send()
-            for side, goes in ((1, goes_down), (2, goes_up)):
-                @pl.when(goes)
-                def _():
-                    last_waits(side, LAT, 0).wait_send()
 
         real, imag = along_y(state[0].reshape(HALF, N), state[1].reshape(HALF, N), rows, 1)
         real = real.reshape(LEVELS, 2, ROWS, N)
@@ -572,6 +561,17 @@
         return 0
 
     lax.fori_loop(0, TICKS, one_tick, 0)
+    last_waits(0, LAT - 1, 0).wait_send()
+    for side, edge_level, beyond in ((0, LEVELS - 1, has_below), (1, 0, has_above)):
+        @pl.when(jnp.logical_or(beyond, level != edge_level))
+        def _():
+            for tick in range(last):
+                group_back_waits(tick, side).wait_send()
+
+        @pl.when(jnp.logical_and(beyond, level == edge_level))
+        def _():
+            last_waits(1 + side, LAT, 0).wait_send()
+
     remote(
         got_there.at[0, pl.ds(0, LAT - 1)], got_there.at[0, pl.ds(0, LAT - 1)],
         there_send.at[0], there_recv.at[0], neighbour,

time: 42.3 us -> 42.4 us (level)
  no operation moved by 1% of the time
where the time goes in v5:
time: 42.4 us; the launch traced here: 42.3 us
  Pallas kernels  41.7 us (98%)
  between operations  0.64 us (2%)
    pallas_call x1, Pallas kernels, step(): pl.pallas_call(kernel, out_shape=pltpu.VMEM((2, LEVELS, 2, ROWS, N), f32)...  41 us

profile of v5, /device:TPU:1, one launch (start us, length us, event | category | flops | bytes accessed | tf_op | source)
XLA Modules:
  0.0 42.3 jit_solution(343867284035517706)
XLA Ops:
  0.6 41.0 %shard_map.138.state = f32[2,4,2,8,256]{4,3,2,1,0:T(8,128)S(1)} custom-call(f32[4,8,256]{2,1,0:T(8,128)} %down_real.1, f32[4,8,256]{2,1,0:T(8,128)} %down_imag.1, f32[4,8,256]{2,1,0:T(8,128)} %up_real.1, f32[4,8,256]{2,1,0:T(8,128)} %up_imag.1, f32[4,8,256]{2,1,0:T(8,128)} %slowness.1, f32[4]{0:T(128)} %ref_slow.1, f32[4,8,256]{2,1,0:T(8,128)} %reflect.1, ...), custom_call_target="tpu_custom_call" | custom-call | tf_op jit(solution)/shard_map/pallas_call | solution.py:626
  41.6 0.7 %shard_map.139 = (f32[4,8,256]{2,1,0:T(8,128)}, f32[4,8,256]{2,1,0:T(8,128)}, f32[4,8,256]{2,1,0:T(8,128)}, f32[4,8,256]{2,1,0:T(8,128)}) custom-call(f32[2,4,2,8,256]{4,3,2,1,0:T(8,128)S(1)} %shard_map.138.state), custom_call_target="tpu_custom_call" | custom-call | tf_op jit(solution)/shard_map/pallas_call | solution.py:653

commit v6 on v4

--- a/solution.py
+++ b/solution.py
@@ -361,7 +361,7 @@
             ).start()
             return 0
 
-        lax.fori_loop(1, GROUP, send, 0)
+        lax.fori_loop(1, GROUP, send, 0, unroll=True)
         got_there[tick, pl.ds(LEVELS * member, LEVELS)] = sent_there[tick, member]
 
     def far_member(to_block):
@@ -397,7 +397,7 @@
 
             return 0
 
-        lax.fori_loop(0, GROUP, send, 0)
+        lax.fori_loop(0, GROUP, send, 0, unroll=True)
         return goes_down, goes_up
 
     def group_back_waits(tick, side):

time: 42.3 us -> 42.1 us (level)
  no operation moved by 1% of the time
where the time goes in v6:
time: 42.1 us; the launch traced here: 42 us
  Pallas kernels  41.3 us (98%)
  between operations  0.64 us (2%)
    pallas_call x1, Pallas kernels, step(): pl.pallas_call(kernel, out_shape=pltpu.VMEM((2, LEVELS, 2, ROWS, N), f32)...  40.6 us

profile of v6, /device:TPU:1, one launch (start us, length us, event | category | flops | bytes accessed | tf_op | source)
XLA Modules:
  0.0 42.0 jit_solution(16043622612193147090)
XLA Ops:
  0.6 40.6 %shard_map.138.state = f32[2,4,2,8,256]{4,3,2,1,0:T(8,128)S(1)} custom-call(f32[4,8,256]{2,1,0:T(8,128)} %down_real.1, f32[4,8,256]{2,1,0:T(8,128)} %down_imag.1, f32[4,8,256]{2,1,0:T(8,128)} %up_real.1, f32[4,8,256]{2,1,0:T(8,128)} %up_imag.1, f32[4,8,256]{2,1,0:T(8,128)} %slowness.1, f32[4]{0:T(128)} %ref_slow.1, f32[4,8,256]{2,1,0:T(8,128)} %reflect.1, ...), custom_call_target="tpu_custom_call" | custom-call | tf_op jit(solution)/shard_map/pallas_call | solution.py:626
  41.3 0.7 %shard_map.139 = (f32[4,8,256]{2,1,0:T(8,128)}, f32[4,8,256]{2,1,0:T(8,128)}, f32[4,8,256]{2,1,0:T(8,128)}, f32[4,8,256]{2,1,0:T(8,128)}) custom-call(f32[2,4,2,8,256]{4,3,2,1,0:T(8,128)S(1)} %shard_map.138.state), custom_call_target="tpu_custom_call" | custom-call | tf_op jit(solution)/shard_map/pallas_call | solution.py:653
